TPU v7x, 32 devices: a whole 2x2x4 slice. The times are simulated.
32 devices in a mesh: dp: 16 (over z, y, x), mp: 2 (over core).
Axes of the slice: x: 2, y: 2, z: 4, core: 2. Of those that a mesh axis runs over, the one named last changes fastest.
Arguments:
- hidden_in: bfloat16 [2048, 2048], P('dp'), may hold values from -6 to 6
- depth: int32 [2048], P('dp'), may hold values from 1 to 3
- destination: int32 [3, 2048], P(None, 'dp'), may hold values from 0 to 2047, as said below
- weight: bfloat16 [2048, 2048], P('dp', 'mp'), may hold values from -0.125 to 0.125
- cotangent: bfloat16 [2048, 2048], P('dp'), may hold values from -6 to 6
Outputs:
- final: bfloat16 [2048, 2048], P('dp')
- grad_in: bfloat16 [2048, 2048], P('dp')
- grad_weight: float32 [2048, 2048], P('dp', 'mp')
Inputs may be any that keep to these rules, and one draw needn't show every extreme that they name: For each recursion, destination is a permutation of the 2048 rows; position p lies on device p // 128. The rows of one device go to 8 devices, exactly 16 rows to each.
All inputs are finite; a program needn't handle non-finite values.
Results may differ from a plain program's by a relative error of at most 0.017.
Values may be sent and summed in bfloat16 or wider, within the bound.
A program may use at most 128 MiB of HBM per device.

v0:
```python
import jax
import jax.numpy as jnp
from jax import lax
from jax.sharding import PartitionSpec as P


def unpack_tags(tag_in, rows):
    tag_f = tag_in.astype(jnp.float32)
    landed = (tag_f[:, 0] * 64.0 + tag_f[:, 1]).astype(jnp.int32)
    level_in = tag_f[:, 2]
    valid = level_in > 0.5
    index = jnp.where(valid, landed, rows)
    return (index, level_in, valid)


def body(hidden_in, depth, destination, weight, cotangent):
    rows, width = hidden_in.shape
    groups = lax.axis_size("dp")
    cap = max(2, 2 * rows // groups)
    slots_all = groups * cap
    gathered = lax.all_gather(weight, "dp", axis=0, tiled=True)
    state = hidden_in
    levels = depth.astype(jnp.float32)
    saved = []
    for step in range(3):
        target = destination[step]
        device_of = target // rows
        slot_of = target % rows
        onehot = (device_of[:, None] == jnp.arange(groups, dtype=jnp.int32)[None, :]).astype(
            jnp.int32
        )
        rank = jnp.sum((jnp.cumsum(onehot, axis=0) - onehot) * onehot, axis=1)
        place = device_of * cap + rank
        tags = jnp.stack(
            [(slot_of // 64).astype(jnp.float32), (slot_of % 64).astype(jnp.float32), levels],
            axis=1,
        ).astype(jnp.bfloat16)
        tag_buf = jnp.zeros((slots_all, 3), jnp.bfloat16).at[place].set(tags)
        data_buf = jnp.zeros((slots_all, width), jnp.bfloat16).at[place].set(state)
        data_in, tag_in = (
            lax.all_to_all(data_buf, "dp", split_axis=0, concat_axis=0, tiled=True),
            lax.all_to_all(tag_buf, "dp", split_axis=0, concat_axis=0, tiled=True),
        )
        index, level_in, valid = unpack_tags(tag_in, rows)
        state = jnp.zeros((rows, width), jnp.bfloat16).at[index].set(data_in, mode="drop")
        levels = jnp.zeros((rows,), jnp.float32).at[index].set(level_in, mode="drop")
        state_f = state.astype(jnp.float32)
        rinv = lax.rsqrt(jnp.mean(state_f * state_f, axis=-1, keepdims=True) + 1e-06)
        normed = (state_f * rinv).astype(jnp.bfloat16)
        inner = jnp.dot(normed, gathered, preferred_element_type=jnp.float32)
        gated = jax.nn.silu(inner).astype(jnp.bfloat16)
        branch = lax.psum(
            jnp.dot(gated, gathered.T, preferred_element_type=jnp.float32).astype(jnp.bfloat16),
            "mp",
        ).astype(jnp.float32)
        active = (levels >= step + 1).astype(jnp.float32)[:, None]
        saved.append((state_f, rinv, normed, inner, gated, active, index, valid, place))
        state = (state_f + active * branch).astype(jnp.bfloat16)
    backward_weight = lax.all_gather(weight, "dp", axis=0, tiled=True)
    grad_state = cotangent.astype(jnp.float32)
    grad_weight = jnp.zeros((width, backward_weight.shape[1]), jnp.float32)
    contract_rows = (((0,), (0,)), ((), ()))
    for step in (2, 1, 0):
        state_f, rinv, normed, inner, gated, active, index, valid, place = saved[step]
        grad_branch = (active * grad_state).astype(jnp.bfloat16)
        grad_gated = jnp.dot(grad_branch, backward_weight, preferred_element_type=jnp.float32)
        sigma = jax.nn.sigmoid(inner)
        grad_inner = (grad_gated * sigma * (1.0 + inner * (1.0 - sigma))).astype(jnp.bfloat16)
        grad_normed = lax.psum(
            jnp.dot(grad_inner, backward_weight.T, preferred_element_type=jnp.float32).astype(
                jnp.bfloat16
            ),
            "mp",
        ).astype(jnp.float32)
        inner_mean = jnp.mean(grad_normed * state_f, axis=-1, keepdims=True)
        grad_entry = grad_state + rinv * grad_normed - state_f * rinv * rinv * rinv * inner_mean
        grad_weight = (
            grad_weight
            + lax.dot_general(normed, grad_inner, contract_rows, preferred_element_type=jnp.float32)
            + lax.dot_general(grad_branch, gated, contract_rows, preferred_element_type=jnp.float32)
        )
        entry_low = grad_entry.astype(jnp.bfloat16)
        safe_index = jnp.minimum(index, rows - 1)
        back_buf = jnp.where(valid[:, None], entry_low[safe_index], jnp.zeros((), jnp.bfloat16))
        returned = lax.all_to_all(back_buf, "dp", split_axis=0, concat_axis=0, tiled=True)
        grad_low = returned[place]
        grad_state = grad_low.astype(jnp.float32)
    grad_in = grad_state.astype(jnp.bfloat16)
    grad_owned = lax.psum_scatter(grad_weight, "dp", scatter_dimension=0, tiled=True)
    return (state, grad_in, grad_owned)


def solution(mesh):
    placed = (P("dp", None), P("dp"), P(None, "dp"), P("dp", "mp"), P("dp", None))
    return jax.shard_map(
        body,
        mesh=mesh,
        in_specs=placed,
        out_specs=(P("dp", None), P("dp", None), P("dp", "mp")),
        check_vma=False,
    )
```

profile of v0, /device:TPU:0, one launch (start us, length us, event | category | flops | bytes accessed | tf_op | source)
XLA Modules:
  0.0 585.1 jit_solution(13903415850796789991)
XLA Ops:
  14.0 8.3 %all-to-all-start = ((bf16[16,16,3]{1,2,0:T(4,128)(2,1)}), bf16[16,16,3]{1,2,0:T(4,128)(2,1)S(1)}, u32[]{:S(2)}, u32[]{:S(2)}) async-start(bf16[16,16,3]{1,2,0:T(4,128)(2,1)} %copy.33), calls=%async_computation | async-start | bytes 32768 | tf_op jit(solution)/shard_map/all_to_all | solution.py:42
  22.3 3.0 scatter_custom_fusion.5
  25.3 4.3 all-to-all-done
  29.7 3.7 all-to-all-start.3
  34.9 32.8 %all-to-all-done.3 = bf16[16,16,2048]{2,1,0:T(8,128)(2,1)S(1)} async-done(((bf16[16,16,2048]{2,1,0:T(8,128)(2,1)}), bf16[16,16,2048]{2,1,0:T(8,128)(2,1)S(1)}, u32[]{:S(2)}, u32[]{:S(2)}) %all-to-all-start.3) | async-done | bytes 1048608 | tf_op jit(solution)/shard_map/all_to_all | solution.py:41
  67.7 2.2 scatter_custom_fusion.6
  70.1 29.7 %all-gather.2.cloned.1.call-done = bf16[2048,1024]{1,0:T(8,128)(2,1)} async-done(((bf16[128,1024]{1,0:T(8,128)(2,1)}), bf16[2048,1024]{1,0:T(8,128)(2,1)}) %all-gather.2.cloned.1.call-update) | async-done | bytes 4194320 | tf_op jit(solution)/shard_map/all_gather | solution.py:21
  99.8 3.1 fusion.70
  103.7 2.3 convolution_convert_fusion.5
  107.9 4.2 all-to-all-start.1
  112.1 11.4 %all-reduce.7.cloned.1.call-done = bf16[128,2048]{1,0:T(8,128)(2,1)} async-done(((bf16[128,2048]{1,0:T(8,128)(2,1)}), bf16[128,2048]{1,0:T(8,128)(2,1)}) %all-reduce.7.cloned.1.call-update) | async-done | bytes 524304 | tf_op jit(solution)/shard_map/psum | solution.py:52
  123.5 3.1 scatter_custom_fusion.7
  126.6 6.8 %all-to-all-start.4 = ((bf16[16,16,2048]{2,1,0:T(8,128)(2,1)}), bf16[16,16,2048]{2,1,0:T(8,128)(2,1)S(1)}, u32[]{:S(2)}, u32[]{:S(2)}) async-start(bf16[16,16,2048]{2,1,0:T(8,128)(2,1)} %bitcast.25), calls=%async_computation.4 | async-start | bytes 2097152 | tf_op jit(solution)/shard_map/all_to_all | solution.py:41
  133.6 1.6 scatter_custom_fusion.3
  135.2 22.9 %all-to-all-done.4 = bf16[16,16,2048]{2,1,0:T(8,128)(2,1)S(1)} async-done(((bf16[16,16,2048]{2,1,0:T(8,128)(2,1)}), bf16[16,16,2048]{2,1,0:T(8,128)(2,1)S(1)}, u32[]{:S(2)}, u32[]{:S(2)}) %all-to-all-start.4) | async-done | bytes 1048608 | tf_op jit(solution)/shard_map/all_to_all | solution.py:41
  158.1 2.2 scatter_custom_fusion.8
  160.5 3.1 fusion.66
  163.7 2.3 convolution_convert_fusion.4
  167.9 6.5 %all-to-all-start.2 = ((bf16[16,16,3]{1,2,0:T(4,128)(2,1)}), bf16[16,16,3]{1,2,0:T(4,128)(2,1)S(1)}, u32[]{:S(2)}, u32[]{:S(2)}) async-start(bf16[16,16,3]{1,2,0:T(4,128)(2,1)} %copy.39), calls=%async_computation.2 | async-start | bytes 32768 | tf_op jit(solution)/shard_map/all_to_all | solution.py:42
  174.5 11.4 %all-reduce.9.cloned.1.call-done = bf16[128,2048]{1,0:T(8,128)(2,1)} async-done(((bf16[128,2048]{1,0:T(8,128)(2,1)}), bf16[128,2048]{1,0:T(8,128)(2,1)}) %all-reduce.9.cloned.1.call-update) | async-done | bytes 524304 | tf_op jit(solution)/shard_map/psum | solution.py:52
  185.9 3.1 scatter_custom_fusion.9
  189.0 7.0 %all-to-all-start.5 = ((bf16[16,16,2048]{2,1,0:T(8,128)(2,1)}), bf16[16,16,2048]{2,1,0:T(8,128)(2,1)}, u32[]{:S(2)}, u32[]{:S(2)}) async-start(bf16[16,16,2048]{2,1,0:T(8,128)(2,1)} %bitcast.27), calls=%async_computation.5 | async-start | bytes 2097152 | tf_op jit(solution)/shard_map/all_to_all | solution.py:41
  197.6 23.1 %all-to-all-done.5 = bf16[16,16,2048]{2,1,0:T(8,128)(2,1)} async-done(((bf16[16,16,2048]{2,1,0:T(8,128)(2,1)}), bf16[16,16,2048]{2,1,0:T(8,128)(2,1)}, u32[]{:S(2)}, u32[]{:S(2)}) %all-to-all-start.5) | async-done | bytes 1048608 | tf_op jit(solution)/shard_map/all_to_all | solution.py:41
  220.7 3.1 scatter_custom_fusion.10
  224.0 3.1 fusion.62
  228.9 2.3 convolution_convert_fusion.2
  231.3 19.7 %all-reduce.11.cloned.1.call-done = bf16[128,2048]{1,0:T(8,128)(2,1)} async-done(((bf16[128,2048]{1,0:T(8,128)(2,1)}), bf16[128,2048]{1,0:T(8,128)(2,1)}) %all-reduce.11.cloned.1.call-update) | async-done | bytes 524304 | tf_op jit(solution)/shard_map/psum | solution.py:69
  256.2 6.8 %all-to-all-start.6 = ((bf16[16,16,2048]{2,1,0:T(8,128)(2,1)}), bf16[16,16,2048]{2,1,0:T(8,128)(2,1)S(1)}, u32[]{:S(2)}, u32[]{:S(2)}) async-start(bf16[16,16,2048]{2,1,0:T(8,128)(2,1)} %broadcast_select_fusion), calls=%async_computation.6 | async-start | bytes 2097152 | tf_op jit(solution)/shard_map/all_to_all | solution.py:85
  263.1 24.6 %all-to-all-done.6 = bf16[16,16,2048]{2,1,0:T(8,128)(2,1)S(1)} async-done(((bf16[16,16,2048]{2,1,0:T(8,128)(2,1)}), bf16[16,16,2048]{2,1,0:T(8,128)(2,1)S(1)}, u32[]{:S(2)}, u32[]{:S(2)}) %all-to-all-start.6) | async-done | bytes 1048608 | tf_op jit(solution)/shard_map/all_to_all | solution.py:85
  288.6 3.4 fusion.10
  292.4 2.3 convolution_convert_fusion.1
  294.9 19.7 %all-reduce.13.cloned.1.call-done = bf16[128,2048]{1,0:T(8,128)(2,1)} async-done(((bf16[128,2048]{1,0:T(8,128)(2,1)}), bf16[128,2048]{1,0:T(8,128)(2,1)}) %all-reduce.13.cloned.1.call-update) | async-done | bytes 524304 | tf_op jit(solution)/shard_map/psum | solution.py:69
  315.8 1.6 fusion.19
  320.0 6.8 %all-to-all-start.7 = ((bf16[16,16,2048]{2,1,0:T(8,128)(2,1)}), bf16[16,16,2048]{2,1,0:T(8,128)(2,1)S(1)}, u32[]{:S(2)}, u32[]{:S(2)}) async-start(bf16[16,16,2048]{2,1,0:T(8,128)(2,1)} %broadcast_select_fusion.1), calls=%async_computation.7 | async-start | bytes 2097152 | tf_op jit(solution)/shard_map/all_to_all | solution.py:85
  327.1 4.5 convolution_convert_fusion.3
  331.6 4.6 fusion.60
  336.2 4.6 fusion.57
  340.7 4.6 fusion.64
  345.3 4.6 fusion.54
  352.4 3.1 fusion.9
  355.4 4.6 fusion.68
  360.0 2.3 convolution_convert_fusion
  362.7 18.4 %add_add_fusion = f32[2048,1024]{1,0:T(8,128)} fusion(f32[2048,1024]{1,0:T(8,128)} %fusion.68, f32[2048,1024]{1,0:T(8,128)} %fusion.54, f32[2048,1024]{1,0:T(8,128)} %fusion.64, f32[2048,1024]{1,0:T(8,128)} %fusion.60, f32[2048,1024]{1,0:T(8,128)} %fusion.57, bf16[128,2048]{1,0:T(8,128)(2,1)S(1)} %gather_fusion.3, f32[128]{0:T(128)S(1)} %compare_convert_fusion.2, ...), kind=kOutput, calls=%fused_computation.18 | convolution fusion | flops 548798464 | bytes 51380736 | tf_op jit(solution)/shard_map/dot_general | solution.py:80
  381.2 1.9 all-reduce.15.cloned.1.call-done
  388.3 6.8 %all-to-all-start.8 = ((bf16[16,16,2048]{2,1,0:T(8,128)(2,1)}), bf16[16,16,2048]{2,1,0:T(8,128)(2,1)S(1)}, u32[]{:S(2)}, u32[]{:S(2)}) async-start(bf16[16,16,2048]{2,1,0:T(8,128)(2,1)} %broadcast_select_fusion.2), calls=%async_computation.8 | async-start | bytes 2097152 | tf_op jit(solution)/shard_map/all_to_all | solution.py:85
  396.1 33.9 %all-to-all-done.8 = bf16[16,16,2048]{2,1,0:T(8,128)(2,1)S(1)} async-done(((bf16[16,16,2048]{2,1,0:T(8,128)(2,1)}), bf16[16,16,2048]{2,1,0:T(8,128)(2,1)S(1)}, u32[]{:S(2)}, u32[]{:S(2)}) %all-to-all-start.8) | async-done | bytes 1048608 | tf_op jit(solution)/shard_map/all_to_all | solution.py:85
  430.0 1.7 gather_fusion.5
  431.7 146.0 %reduce-scatter.2.cloned.1.call-done = f32[128,1024]{1,0:T(8,128)} async-done(((f32[2048,1024]{1,0:T(8,128)}), f32[128,1024]{1,0:T(8,128)}) %reduce-scatter.2.cloned.1.call-update) | async-done | bytes 524304 | tf_op jit(solution)/shard_map/reduce_scatter | solution.py:89
  (137 shorter events, 37.2 us)
Async XLA Ops:
  7.2 92.6 %all-gather.2.cloned.1.call-start = ((), (), s32[]{:S(2)}) async-start(), calls=%async_computation.10 | async-start | bytes 4456448 | tf_op jit(solution)/shard_map/all_gather | solution.py:21
  14.0 15.7 %all-to-all-start = ((bf16[16,16,3]{1,2,0:T(4,128)(2,1)}), bf16[16,16,3]{1,2,0:T(4,128)(2,1)S(1)}, u32[]{:S(2)}, u32[]{:S(2)}) async-start(bf16[16,16,3]{1,2,0:T(4,128)(2,1)} %copy.33), calls=%async_computation | async-start | bytes 32768 | tf_op jit(solution)/shard_map/all_to_all | solution.py:42
  29.7 38.1 %all-to-all-start.3 = ((bf16[16,16,2048]{2,1,0:T(8,128)(2,1)}), bf16[16,16,2048]{2,1,0:T(8,128)(2,1)S(1)}, u32[]{:S(2)}, u32[]{:S(2)}) async-start(bf16[16,16,2048]{2,1,0:T(8,128)(2,1)} %bitcast.23), calls=%async_computation.3 | async-start | bytes 2097152 | tf_op jit(solution)/shard_map/all_to_all | solution.py:41
  33.3 90.2 %all-reduce.7.cloned.1.call-start = ((), (), s32[]{:S(2)}) async-start(), calls=%async_computation.11 | async-start | bytes 1048576 | tf_op jit(solution)/shard_map/psum | solution.py:52
  99.8 3.9 copy-start
  102.9 0.8 copy-start.13
  107.9 18.7 %all-to-all-start.1 = ((bf16[16,16,3]{1,2,0:T(4,128)(2,1)}), bf16[16,16,3]{1,2,0:T(4,128)(2,1)S(1)}, u32[]{:S(2)}, u32[]{:S(2)}) async-start(bf16[16,16,3]{1,2,0:T(4,128)(2,1)} %copy.36), calls=%async_computation.1 | async-start | bytes 32768 | tf_op jit(solution)/shard_map/all_to_all | solution.py:42
  126.6 31.5 %all-to-all-start.4 = ((bf16[16,16,2048]{2,1,0:T(8,128)(2,1)}), bf16[16,16,2048]{2,1,0:T(8,128)(2,1)S(1)}, u32[]{:S(2)}, u32[]{:S(2)}) async-start(bf16[16,16,2048]{2,1,0:T(8,128)(2,1)} %bitcast.25), calls=%async_computation.4 | async-start | bytes 2097152 | tf_op jit(solution)/shard_map/all_to_all | solution.py:41
  133.4 52.5 %all-reduce.9.cloned.1.call-start = ((), (), s32[]{:S(2)}) async-start(), calls=%async_computation.12 | async-start | bytes 1048576 | tf_op jit(solution)/shard_map/psum | solution.py:52
  160.3 3.5 copy-start.1
  163.7 25.2 %copy-start.9 = (f32[128,1024]{1,0:T(8,128)}, f32[128,1024]{1,0:T(8,128)S(1)}, u32[]{:S(2)}) copy-start(f32[128,1024]{1,0:T(8,128)S(1)} %fusion.66) | copy-start | bytes 1572868
  167.9 21.0 %all-to-all-start.2 = ((bf16[16,16,3]{1,2,0:T(4,128)(2,1)}), bf16[16,16,3]{1,2,0:T(4,128)(2,1)S(1)}, u32[]{:S(2)}, u32[]{:S(2)}) async-start(bf16[16,16,3]{1,2,0:T(4,128)(2,1)} %copy.39), calls=%async_computation.2 | async-start | bytes 32768 | tf_op jit(solution)/shard_map/all_to_all | solution.py:42
  189.0 38.9 %copy-start.7 = (bf16[128,2048]{1,0:T(8,128)(2,1)S(1)}, bf16[128,2048]{1,0:T(8,128)(2,1)}, u32[]{:S(2)}) copy-start(bf16[128,2048]{1,0:T(8,128)(2,1)} %param.9) | copy-start | bytes 1572868
  189.0 31.7 %all-to-all-start.5 = ((bf16[16,16,2048]{2,1,0:T(8,128)(2,1)}), bf16[16,16,2048]{2,1,0:T(8,128)(2,1)}, u32[]{:S(2)}, u32[]{:S(2)}) async-start(bf16[16,16,2048]{2,1,0:T(8,128)(2,1)} %bitcast.27), calls=%async_computation.5 | async-start | bytes 2097152 | tf_op jit(solution)/shard_map/all_to_all | solution.py:41
  196.0 55.0 %all-reduce.11.cloned.1.call-start = ((), (), s32[]{:S(2)}) async-start(), calls=%async_computation.13 | async-start | bytes 1048576 | tf_op jit(solution)/shard_map/psum | solution.py:69
  223.8 4.1 copy-start.2
  227.1 0.8 copy-start.11
  256.2 31.5 %all-to-all-start.6 = ((bf16[16,16,2048]{2,1,0:T(8,128)(2,1)}), bf16[16,16,2048]{2,1,0:T(8,128)(2,1)S(1)}, u32[]{:S(2)}, u32[]{:S(2)}) async-start(bf16[16,16,2048]{2,1,0:T(8,128)(2,1)} %broadcast_select_fusion), calls=%async_computation.6 | async-start | bytes 2097152 | tf_op jit(solution)/shard_map/all_to_all | solution.py:85
  263.0 51.5 %all-reduce.13.cloned.1.call-start = ((), (), s32[]{:S(2)}) async-start(), calls=%async_computation.14 | async-start | bytes 1048576 | tf_op jit(solution)/shard_map/psum | solution.py:69
  288.6 6.1 %copy-start.5 = (bf16[128,2048]{1,0:T(8,128)(2,1)}, bf16[128,2048]{1,0:T(8,128)(2,1)S(1)}, u32[]{:S(2)}) copy-start(bf16[128,2048]{1,0:T(8,128)(2,1)S(1)} %gather_fusion.1) | copy-start | bytes 1572868
  288.6 3.8 copy-start.3
  292.4 23.4 %copy-start.15 = (bf16[128,1024]{1,0:T(8,128)(2,1)}, bf16[128,1024]{1,0:T(8,128)(2,1)S(1)}, u32[]{:S(2)}) copy-start(bf16[128,1024]{1,0:T(8,128)(2,1)S(1)} %fusion.10) | copy-start | bytes 786436
  318.8 8.2 %copy-start.12 = (f32[128,1024]{1,0:T(8,128)S(1)}, f32[128,1024]{1,0:T(8,128)}, u32[]{:S(2)}) copy-start(f32[128,1024]{1,0:T(8,128)} %copy-done.11) | copy-start | bytes 1572868
  320.0 31.5 %all-to-all-start.7 = ((bf16[16,16,2048]{2,1,0:T(8,128)(2,1)}), bf16[16,16,2048]{2,1,0:T(8,128)(2,1)S(1)}, u32[]{:S(2)}, u32[]{:S(2)}) async-start(bf16[16,16,2048]{2,1,0:T(8,128)(2,1)} %broadcast_select_fusion.1), calls=%async_computation.7 | async-start | bytes 2097152 | tf_op jit(solution)/shard_map/all_to_all | solution.py:85
  326.8 56.3 %all-reduce.15.cloned.1.call-start = ((), (), s32[]{:S(2)}) async-start(), calls=%async_computation.16 | async-start | bytes 2097152 | tf_op jit(solution)/shard_map/psum | solution.py:52
  331.6 4.6 copy-start.8
  336.2 4.6 copy-start.16
  340.7 4.6 copy-start.6
  340.7 4.6 copy-start.10
  349.9 2.5 copy-start.14
  355.4 4.6 copy-start.4
  362.3 215.4 %reduce-scatter.2.cloned.1.call-start = ((), (), s32[]{:S(2)}) async-start(), calls=%async_computation.15 | async-start | bytes 8912896 | tf_op jit(solution)/shard_map/reduce_scatter | solution.py:89
  387.2 8.0 %copy-start.17 = (bf16[128,2048]{1,0:T(8,128)(2,1)S(1)}, bf16[128,2048]{1,0:T(8,128)(2,1)}, u32[]{:S(2)}) copy-start(bf16[128,2048]{1,0:T(8,128)(2,1)} %get-tuple-element.3) | copy-start | bytes 1572868
  388.3 41.7 %all-to-all-start.8 = ((bf16[16,16,2048]{2,1,0:T(8,128)(2,1)}), bf16[16,16,2048]{2,1,0:T(8,128)(2,1)S(1)}, u32[]{:S(2)}, u32[]{:S(2)}) async-start(bf16[16,16,2048]{2,1,0:T(8,128)(2,1)} %broadcast_select_fusion.2), calls=%async_computation.8 | async-start | bytes 2097152 | tf_op jit(solution)/shard_map/all_to_all | solution.py:85
Sparse Core Ops, SparseCore 0:
  10.8 88.9 all-gather.1
  106.2 17.3 all-reduce.6
  166.2 19.6 all-reduce.8
  231.3 19.6 all-reduce.10
  294.9 19.6 all-reduce.12
  362.5 20.5 all-reduce.14
  386.0 191.6 reduce-scatter.1
where the time goes:
time: 596 us; the launch traced here: 585 us
  waiting for transfers between devices  384 us (64%)
  matrix products  74 us (12%)
  starting transfers between devices  57.7 us (10%)
  local copies, waits for them, and re-layouts  30.6 us (5%)
  other arithmetic  24 us (4%)
  between operations  15.2 us (3%)
    reduce_scatter x1, waiting for transfers between devices, body(): lax.psum_scatter(grad_weight, 'dp', scatter_dimension=0, tiled=True)  146 us
    all_to_all x3, waiting for transfers between devices, body(): lax.all_to_all(data_buf, 'dp', split_axis=0, concat_axis=0, tiled=True)  78.8 us
    all_to_all x3, waiting for transfers between devices, body(): lax.all_to_all(back_buf, 'dp', split_axis=0, concat_axis=0, tiled=True)  60 us
    psum x2, waiting for transfers between devices, body(): lax.psum(jnp.dot(grad_inner, backward_weight.T, preferred_element_type=jn...  39.3 us
    all_gather x1, waiting for transfers between devices, body(): gathered = lax.all_gather(weight, 'dp', axis=0, tiled=True)  29.7 us
    dot_general x3, matrix products, body(): lax.dot_general(grad_branch, gated, contract_rows, preferred_element_type...  27.5 us
    psum x3, waiting for transfers between devices, body(): lax.psum(jnp.dot(gated, gathered.T, preferred_element_type=jnp.float32).a...  24.7 us
    all_to_all x3, starting transfers between devices, body(): lax.all_to_all(back_buf, 'dp', split_axis=0, concat_axis=0, tiled=True)  20.4 us
  transfers between devices with their start and end apart: 16, of which 14 were waited for; matrix products, arithmetic and copies ran while one was open for 13% of the time, Pallas kernels for 0%

commit v1 on v0

v1 whole, which is shorter than its diff:
```python
import jax
import jax.numpy as jnp
from jax import lax
from jax.sharding import PartitionSpec as P


def pick(table, index):
    ids = lax.broadcasted_iota(jnp.int32, (index.shape[0], table.shape[0]), 1)
    return jnp.sum(jnp.where(ids == index[:, None], table[None, :], 0), axis=1)


def find(table, value):
    ids = lax.broadcasted_iota(jnp.int32, (value.shape[0], table.shape[0]), 1)
    return jnp.sum(jnp.where(table[None, :] == value[:, None], ids, 0), axis=1)


def take_rows(index, table):
    ids = lax.broadcasted_iota(jnp.int32, (index.shape[0], table.shape[0]), 1)
    return jnp.dot(
        (ids == index[:, None]).astype(jnp.bfloat16), table, preferred_element_type=jnp.float32
    ).astype(jnp.bfloat16)


def recursions(state, levels, cot, weight):
    saved = []
    for step in range(3):
        state_f = state.astype(jnp.float32)
        rinv = lax.rsqrt(jnp.mean(state_f * state_f, axis=-1, keepdims=True) + 1e-06)
        normed = (state_f * rinv).astype(jnp.bfloat16)
        inner = jnp.dot(normed, weight, preferred_element_type=jnp.float32)
        gated = jax.nn.silu(inner).astype(jnp.bfloat16)
        branch = lax.dot_general(
            gated, weight, (((1,), (1,)), ((), ())), preferred_element_type=jnp.float32
        )
        active = (levels >= step + 1).astype(jnp.float32)[:, None]
        saved.append((state_f, rinv, normed, inner, gated, active))
        state = (state_f + active * branch).astype(jnp.bfloat16)
    final = state
    grad = cot.astype(jnp.float32)
    lefts, rights = [], []
    for step in (2, 1, 0):
        state_f, rinv, normed, inner, gated, active = saved[step]
        grad_branch = (active * grad).astype(jnp.bfloat16)
        grad_gated = jnp.dot(grad_branch, weight, preferred_element_type=jnp.float32)
        sigma = jax.nn.sigmoid(inner)
        grad_inner = (grad_gated * sigma * (1.0 + inner * (1.0 - sigma))).astype(jnp.bfloat16)
        grad_normed = lax.dot_general(
            grad_inner, weight, (((1,), (1,)), ((), ())), preferred_element_type=jnp.float32
        )
        inner_mean = jnp.mean(grad_normed * state_f, axis=-1, keepdims=True)
        entry = grad + rinv * grad_normed - state_f * rinv * rinv * rinv * inner_mean
        lefts += [normed, grad_branch]
        rights += [grad_inner, gated]
        grad = entry.astype(jnp.bfloat16).astype(jnp.float32)
    return final, grad.astype(jnp.bfloat16), jnp.concatenate(lefts), jnp.concatenate(rights)


def body(hidden_in, depth, destination, weight, cotangent):
    rows, width = hidden_in.shape
    half_inner = weight.shape[1]
    cores = lax.axis_size("mp")
    me, core = lax.axis_index("dp"), lax.axis_index("mp")
    part, strip = rows // cores, width // cores
    columns = lax.all_gather(weight, "dp", axis=0, tiled=True)
    full = lax.all_gather(columns, "mp", axis=1, tiled=True)
    tables = lax.all_gather(destination, "dp", axis=1, tiled=True)
    cot_strip = lax.dynamic_slice_in_dim(cotangent, core * strip, strip, 1)
    cot_all = lax.all_gather(cot_strip, "dp", axis=0, tiled=True)
    place = pick(tables[2], pick(tables[1], destination[0]))
    own = me * rows + jnp.arange(rows, dtype=jnp.int32)
    source = find(tables[0], find(tables[1], find(tables[2], own)))
    cot_rows = lax.all_gather(take_rows(place, cot_all), "mp", axis=1, tiled=True)
    cot = lax.dynamic_slice_in_dim(cot_rows, core * part, part, 0)
    state = lax.dynamic_slice_in_dim(hidden_in, core * part, part, 0)
    levels = lax.dynamic_slice_in_dim(depth, core * part, part, 0)
    last, grad, left, right = recursions(state, levels, cot, full)
    last_all = lax.all_gather(last, "dp", axis=0, tiled=True)
    owner, offset = source // rows, source % rows
    slot = jnp.where(offset // part == core, owner * part + offset % part, -1)
    final = lax.psum(take_rows(slot, last_all), "mp")
    grad_in = lax.all_gather(grad, "mp", axis=0, tiled=True)
    left_all = lax.all_gather(left, "mp", axis=0, tiled=True)
    right_all = lax.all_gather(right, "mp", axis=0, tiled=True)
    right_half = lax.dynamic_slice_in_dim(right_all, core * half_inner, half_inner, 1)
    grad_weight = lax.dot_general(
        left_all, right_half, (((0,), (0,)), ((), ())), preferred_element_type=jnp.float32
    ).astype(jnp.bfloat16)
    owned = lax.psum_scatter(grad_weight, "dp", scatter_dimension=0, tiled=True)
    return final, grad_in, owned.astype(jnp.float32)


def solution(mesh):
    placed = (P("dp", None), P("dp"), P(None, "dp"), P("dp", "mp"), P("dp", None))
    return jax.shard_map(
        body,
        mesh=mesh,
        in_specs=placed,
        out_specs=(P("dp", None), P("dp", None), P("dp", "mp")),
        check_vma=False,
    )
```

time: 596 us -> 450 us (0.76); the launches traced: 585 us -> 449 us
  waiting for transfers between devices: 384 us -> 322 us
  starting transfers between devices: 57.7 us -> 0.54 us
  blocking collectives: 0 us -> 42.9 us
  local copies, waits for them, and re-layouts: 30.6 us -> 5.45 us
  other arithmetic: 24 us -> 6.34 us
  matrix products: 74 us -> 57.6 us
    all_gather x1 -> x6, waiting for transfers between devices: 29.7 us -> 212 us  [the longest x1 80.6 us: body(): columns = lax.all_gather(weight, 'dp', axis=0, tiled=True)]
    all_to_all x9 -> x0, waiting for transfers between devices: 143 us -> none  [the longest x3 78.8 us: body(): lax.all_to_all(data_buf, 'dp', split_axis=0, concat_axis=0, tiled=True)]
    all_to_all x9 -> x0, starting transfers between devices: 56.9 us -> none  [the longest x3 20.4 us: body(): lax.all_to_all(back_buf, 'dp', split_axis=0, concat_axis=0, tiled=True)]
    reduce_scatter x1, waiting for transfers between devices: 146 us -> 89.9 us  [body(): owned = lax.psum_scatter(grad_weight, 'dp', scatter_dimension=0, tiled=True)]
    psum x5 -> x1, waiting for transfers between devices: 64 us -> 19.5 us  [body(): final = lax.psum(take_rows(slot, last_all), 'mp')]
    all_gather x0 -> x3, blocking collectives: none -> 42.9 us  [the longest x1 38.6 us: body(): tables = lax.all_gather(destination, 'dp', axis=1, tiled=True)]
    scatter x10 -> x0, local copies, waits for them, and re-layouts: 17.5 us -> none  [the longest x3 7.45 us: body(): jnp.zeros((rows, width), jnp.bfloat16).at[index].set(data_in, mode='drop')]
    dot_general x18 -> x15, matrix products: 74 us -> 57.6 us  [the longest x3 13.4 us: recursions(): lax.dot_general(gated, weight, (((1,), (1,)), ((), ())), preferred_elemen...]
  transfers between devices with their start and end apart: 16 -> 8, of which waited for: 14 -> 7; matrix products, arithmetic and copies ran while one was open for 13% -> 9% of each run, Pallas kernels for 0% -> 0%
where the time goes in v1:
time: 450 us; the launch traced here: 449 us
  waiting for transfers between devices  322 us (72%)
  matrix products  57.6 us (13%)
  blocking collectives  42.9 us (10%)
  between operations  14.4 us (3%)
  other arithmetic  6.34 us (1%)
  local copies, waits for them, and re-layouts  5.45 us (1%)
    reduce_scatter x1, waiting for transfers between devices, body(): owned = lax.psum_scatter(grad_weight, 'dp', scatter_dimension=0, tiled=True)  89.9 us
    all_gather x1, waiting for transfers between devices, body(): columns = lax.all_gather(weight, 'dp', axis=0, tiled=True)  80.6 us
    all_gather x1, waiting for transfers between devices, body(): last_all = lax.all_gather(last, 'dp', axis=0, tiled=True)  65.7 us
    all_gather x1, blocking collectives, body(): tables = lax.all_gather(destination, 'dp', axis=1, tiled=True)  38.6 us
    all_gather x1, waiting for transfers between devices, body(): cot_all = lax.all_gather(cot_strip, 'dp', axis=0, tiled=True)  38.1 us
    psum x1, waiting for transfers between devices, body(): final = lax.psum(take_rows(slot, last_all), 'mp')  19.5 us
    all_gather x1, waiting for transfers between devices, body(): full = lax.all_gather(columns, 'mp', axis=1, tiled=True)  14.9 us
    dot_general x3, matrix products, recursions(): lax.dot_general(gated, weight, (((1,), (1,)), ((), ())), preferred_elemen...  13.4 us
  transfers between devices with their start and end apart: 8, of which 7 were waited for; matrix products, arithmetic and copies ran while one was open for 9% of the time, Pallas kernels for 0%

profile of v1, /device:TPU:0, one launch (start us, length us, event | category | flops | bytes accessed | tf_op | source)
XLA Modules:
  0.0 449.3 jit_solution(8646340959882952697)
XLA Ops:
  7.3 0.7 all-gather.7.cloned.1.call-update
  8.0 0.2 copy-done
  8.2 0.7 constant_dynamic-slice_fusion
  9.0 80.6 %all-gather.7.cloned.1.call-done = bf16[2048,1024]{1,0:T(8,128)(2,1)} async-done(((bf16[128,1024]{1,0:T(8,128)(2,1)}), bf16[2048,1024]{1,0:T(8,128)(2,1)}) %all-gather.7.cloned.1.call-update) | async-done | bytes 4194320 | tf_op jit(solution)/shard_map/all_gather | solution.py:64
  89.7 0.2 fusion.28
  89.9 38.6 %all_gather.27 = s32[3,2048]{1,0:T(4,128)S(1)} all-gather(s32[3,128]{1,0:T(4,128)S(1)} %copy-done.7), channel_id=1, replica_groups=mesh['dp'=16,'mp'=2] {'dp'}, dimensions={1}, use_global_device_ids=true | all-gather | bytes 26112 | tf_op jit(solution)/shard_map/all_gather | solution.py:66
  128.6 0.3 select_reduce_fusion.1
  128.8 0.4 select_reduce_fusion
  129.3 38.1 %all-gather.13.cloned.1.call-done = bf16[2048,1024]{1,0:T(8,128)(2,1)} async-done(((bf16[128,1024]{1,0:T(8,128)(2,1)}), bf16[2048,1024]{1,0:T(8,128)(2,1)}) %all-gather.13.cloned.1.call-update) | async-done | bytes 4194320 | tf_op jit(solution)/shard_map/all_gather | solution.py:68
  167.4 2.9 convolution_convert_fusion.2
  170.3 2.2 all_gather.32
  172.5 14.9 %all-gather.9.cloned.1.call-done = bf16[2048,2048]{1,0:T(8,128)(2,1)} async-done(((bf16[2048,1024]{1,0:T(8,128)(2,1)}), bf16[2048,2048]{1,0:T(8,128)(2,1)}) %all-gather.9.cloned.1.call-update) | async-done | bytes 8388624 | tf_op jit(solution)/shard_map/all_gather | solution.py:65
  187.4 5.1 %fusion.39 = f32[64,2048]{1,0:T(8,128)S(1)} fusion(bf16[2048,2048]{1,0:T(8,128)(2,1)} %all-gather.9.cloned.1.call-done, f32[64]{0:T(128)S(1)} %add_rsqrt_fusion.2, bf16[128,2048]{1,0:T(8,128)(2,1)S(1)} %copy-done.2, s32[]{:T(128)S(6)} %select_n.77), kind=kOutput, calls=%fused_computation.75 | convolution fusion | flops 537264128 | bytes 9175556 | tf_op jit(solution)/shard_map/dot_general | solution.py:30
  192.6 0.6 copy-done.1
  193.2 2.8 multiply_reduce_fusion.3
  196.0 1.6 fusion.45
  197.7 2.8 multiply_reduce_fusion.2
  200.5 0.1 constant_dynamic-update-slice_fusion.1
  200.6 0.1 fusion.36
  200.8 1.6 fusion.46
  202.5 1.8 constant_dynamic-update-slice_fusion.7
  204.3 0.1 constant_dynamic-update-slice_fusion.6
  204.4 2.8 multiply_reduce_fusion.1
  207.2 0.3 fusion.34
  207.5 0.1 fusion.38
  207.6 2.0 constant_dynamic-update-slice_fusion.5
  209.6 2.8 multiply_reduce_fusion
  212.3 0.3 fusion.32
  212.6 1.2 copy-done.6
  213.9 0.8 constant_dynamic-update-slice_fusion.4
  214.7 5.8 %constant_dynamic-update-slice_fusion.3 = (bf16[384,2048]{1,0:T(8,128)(2,1)}, bf16[64,2048]{1,0:T(8,128)(2,1)S(1)}) fusion(bf16[384,2048]{1,0:T(8,128)(2,1)} %constant_dynamic-update-slice_fusion.4, f32[64,2048]{1,0:T(8,128)S(1)} %fusion.39, bf16[2048,2048]{1,0:T(8,128)(2,1)} %all-gather.9.cloned.1.call-done, bf16[64,2048]{1,0:T(8,128)(2,1)S(1)} %get-tuple-element.6, ...), kind=kOutput, calls=%fused_computation.79 | convolution fusion | flops 538443776 | bytes 9699584 | tf_op jit(solution)/shard_map/dot_general | solution.py:44
  220.5 0.9 constant_dynamic-update-slice_fusion.2
  221.4 7.9 %fusion.10 = bf16[64,2048]{1,0:T(8,128)(2,1)} fusion(f32[64,2048]{1,0:T(8,128)S(1)} %get-tuple-element.18, bf16[2048,2048]{1,0:T(8,128)(2,1)} %all-gather.9.cloned.1.call-done, f32[64]{0:T(128)S(1)} %get-tuple-element.12, f32[64,2048]{1,0:T(8,128)S(1)} %fusion.46), kind=kOutput, calls=%fused_computation.18 | convolution fusion | flops 537919488 | bytes 9699584 | tf_op jit(solution)/shard_map/dot_general | solution.py:32
  229.4 12.6 %all-gather.17.cloned.1.call-done = bf16[768,2048]{1,0:T(8,128)(2,1)} async-done(((bf16[384,2048]{1,0:T(8,128)(2,1)}), bf16[768,2048]{1,0:T(8,128)(2,1)}) %all-gather.17.cloned.1.call-update) | async-done | bytes 3145744 | tf_op jit(solution)/shard_map/all_gather | solution.py:83
  242.0 7.8 %convolution_convert_fusion = bf16[2048,1024]{1,0:T(8,128)(2,1)} fusion(bf16[768,2048]{1,0:T(8,128)(2,1)} %all-gather.15.cloned.1.call-done, bf16[768,2048]{1,0:T(8,128)(2,1)} %all-gather.17.cloned.1.call-done, s32[]{:T(128)S(6)} %select_n.80), kind=kOutput, calls=%fused_computation | convolution fusion | flops 3223322624 | bytes 8912900 | tf_op jit(solution)/shard_map/dot_general | solution.py:85
  249.8 0.3 all-reduce.2.cloned.1.call-start
  250.0 0.3 select_reduce_fusion.3
  250.3 0.3 select_reduce_fusion.2
  250.6 6.2 %fusion.29 = (f32[64]{0:T(128)S(1)}, f32[64,2048]{1,0:T(8,128)S(1)}) fusion(bf16[128,2048]{1,0:T(8,128)(2,1)S(1)} %copy-done.2, s32[]{:T(128)S(6)} %select_n.77, bf16[64,2048]{1,0:T(8,128)(2,1)S(1)} %get-tuple-element.30, bf16[2048,2048]{1,0:T(8,128)(2,1)} %all-gather.9.cloned.1.call-done), kind=kOutput, calls=%fused_computation.55 | convolution fusion | flops 537264064 | bytes 9437444 | tf_op jit(solution)/shard_map/dot_general | solution.py:47
  256.8 65.7 %all-gather.11.cloned.1.call-done = bf16[1024,2048]{1,0:T(8,128)(2,1)} async-done(((bf16[64,2048]{1,0:T(8,128)(2,1)}), bf16[1024,2048]{1,0:T(8,128)(2,1)}) %all-gather.11.cloned.1.call-update) | async-done | bytes 4194320 | tf_op jit(solution)/shard_map/all_gather | solution.py:77
  322.5 3.7 convolution_convert_fusion.1
  326.2 0.2 fusion.20
  326.5 2.2 all_gather.33
  328.6 89.9 %reduce-scatter.2.cloned.1.call-done = bf16[128,1024]{1,0:T(8,128)(2,1)} async-done(((bf16[2048,1024]{1,0:T(8,128)(2,1)}), bf16[128,1024]{1,0:T(8,128)(2,1)}) %reduce-scatter.2.cloned.1.call-update) | async-done | bytes 262160 | tf_op jit(solution)/shard_map/reduce_scatter | solution.py:88
  418.5 1.8 convert_element_type.127
  420.3 19.5 %all-reduce.2.cloned.1.call-done = bf16[128,2048]{1,0:T(8,128)(2,1)} async-done(((bf16[128,2048]{1,0:T(8,128)(2,1)}), bf16[128,2048]{1,0:T(8,128)(2,1)}) %all-reduce.2.cloned.1.call-update) | async-done | bytes 524304 | tf_op jit(solution)/shard_map/psum | solution.py:80
  439.8 1.9 copy.20
  441.6 0.8 copy.21
  (42 shorter events, 0.7 us)
Async XLA Ops:
  7.2 1.0 copy-start
  7.2 82.5 %copy-start.2 = (bf16[128,2048]{1,0:T(8,128)(2,1)S(1)}, bf16[128,2048]{1,0:T(8,128)(2,1)}, u32[]{:S(2)}) copy-start(bf16[128,2048]{1,0:T(8,128)(2,1)} %param.5) | copy-start | bytes 1572868
  7.2 82.7 %copy-start.7 = (s32[3,128]{1,0:T(4,128)S(1)}, s32[3,128]{1,0:T(4,128)}, u32[]{:S(2)}) copy-start(s32[3,128]{1,0:T(4,128)} %param.7) | copy-start | bytes 4612
  7.2 121.3 %copy-start.8 = (s32[128]{0:T(128)S(1)}, s32[128]{0:T(128)}, u32[]{:S(2)}) copy-start(s32[128]{0:T(128)} %param.6) | copy-start | bytes 1540
  7.2 82.4 %all-gather.7.cloned.1.call-start = ((), (), s32[]{:S(2)}) async-start(), calls=%async_computation.1 | async-start | bytes 4456448 | tf_op jit(solution)/shard_map/all_gather | solution.py:64
  7.9 159.5 %all-gather.13.cloned.1.call-start = ((), (), s32[]{:S(2)}) async-start(), calls=%async_computation.5 | async-start | bytes 4456448 | tf_op jit(solution)/shard_map/all_gather | solution.py:68
  9.0 178.5 %all-gather.9.cloned.1.call-start = ((), (), s32[]{:S(2)}) async-start(), calls=%async_computation.2 | async-start | bytes 12582912 | tf_op jit(solution)/shard_map/all_gather | solution.py:65
  89.7 139.7 %all-gather.15.cloned.1.call-start = ((), (), s32[]{:S(2)}) async-start(), calls=%async_computation.6 | async-start | bytes 4718592 | tf_op jit(solution)/shard_map/all_gather | solution.py:82
  172.5 28.1 %copy-start.3 = (bf16[128,2048]{1,0:T(8,128)(2,1)}, bf16[128,2048]{1,0:T(8,128)(2,1)S(1)}, u32[]{:S(2)}) copy-start(bf16[128,2048]{1,0:T(8,128)(2,1)S(1)} %all_gather.32) | copy-start | bytes 1572868
  187.4 5.8 %copy-start.1 = (bf16[2048,2048]{1,0:T(8,128)(2,1)S(1)}, bf16[2048,2048]{1,0:T(8,128)(2,1)}, u32[]{:S(2)}) copy-start(bf16[2048,2048]{1,0:T(8,128)(2,1)} %all-gather.9.cloned.1.call-done) | copy-start | bytes 25165828
  200.8 1.7 copy-start.4
  209.6 2.8 copy-start.5
  212.6 1.2 copy-start.6
  213.8 28.2 %all-gather.17.cloned.1.call-start = ((), (), s32[]{:S(2)}) async-start(), calls=%async_computation.7 | async-start | bytes 4718592 | tf_op jit(solution)/shard_map/all_gather | solution.py:83
  221.4 101.1 %all-gather.11.cloned.1.call-start = ((), (), s32[]{:S(2)}) async-start(), calls=%async_computation.3 | async-start | bytes 4456448 | tf_op jit(solution)/shard_map/all_gather | solution.py:77
  229.3 189.2 %reduce-scatter.2.cloned.1.call-start = ((), (), s32[]{:S(2)}) async-start(), calls=%async_computation.8 | async-start | bytes 4456448 | tf_op jit(solution)/shard_map/reduce_scatter | solution.py:88
  249.8 190.0 %all-reduce.2.cloned.1.call-start = ((), (), s32[]{:S(2)}) async-start(), calls=%async_computation.4 | async-start | bytes 1048576 | tf_op jit(solution)/shard_map/psum | solution.py:80
Sparse Core Ops, SparseCore 0:
  10.8 78.7 all-gather.6
  93.0 74.3 all-gather.12
  168.9 18.4 all-gather.8
  213.9 13.2 all-gather.14
  228.6 13.2 all-gather.16
  245.2 77.2 all-gather.10
  324.8 93.7 reduce-scatter.1
  421.4 18.2 all-reduce.1

commit v2 on v1

--- a/solution.py
+++ b/solution.py
@@ -1,7 +1,331 @@
 import jax
 import jax.numpy as jnp
 from jax import lax
+from jax.experimental import pallas as pl
+from jax.experimental.pallas import tpu as pltpu
 from jax.sharding import PartitionSpec as P
+
+
+MESH = pl.DeviceIdType.MESH
+
+
+def push(src, dst, send, recv, device):
+    copy = pltpu.make_async_remote_copy(
+        src_ref=src,
+        dst_ref=dst,
+        send_sem=send,
+        recv_sem=recv,
+        device_id=device,
+        device_id_type=MESH,
+    )
+    copy.start()
+
+
+def landed(ref, recv):
+    pltpu.make_async_copy(ref, ref, recv).wait()
+
+
+def place_of(me):
+    return me // 4, (me // 2) % 2, me % 2
+
+
+def greet(z, y, x, core):
+    barrier = pltpu.get_barrier_semaphore()
+
+    def hello(device):
+        pl.semaphore_signal(barrier, inc=1, device_id=device, device_id_type=MESH)
+
+    me = z * 4 + y * 2 + x
+    hello((me, 1 - core))
+    hello((me + 1 - 2 * x, core))
+    hello((me + 2 - 4 * y, core))
+
+    @pl.when(z < 3)
+    def _():
+        hello((me + 4, core))
+
+    @pl.when(z > 0)
+    def _():
+        hello((me - 4, core))
+
+    pl.semaphore_wait(barrier, 3 + (1 - z // 3) + (z + 2) // 3)
+
+
+def gather_kernel(
+    block, out, local, zup, zdn, zrecv, asend, arecv, bsend, brecv, csend, crecv, cas, car, cbs, cbr
+):
+    me, core = lax.axis_index("dp"), lax.axis_index("mp")
+    z, y, x = place_of(me)
+    width = block.shape[1]
+    half = width // 2
+    base = pl.multiple_of(core * width, width)
+    beside = (me, 1 - core)
+    across = ((me + 1 - 2 * x, core), (me + 2 - 4 * y, core))
+    greet(z, y, x, core)
+
+    def cols(h):
+        return pl.ds(pl.multiple_of(core * width + h * half, half), half)
+
+    def whole(zp):
+        return out.at[zp, y, x, :, pl.ds(base, width)]
+
+    def piece(zp, yp, xp, h):
+        return out.at[zp, yp, xp, :, cols(h)]
+
+    def pair(zp, yp, xp, h):
+        if h == 0:
+            return out.at[zp, yp, :, :, cols(0)]
+        return out.at[zp, :, xp, :, cols(1)]
+
+    def spread(zp, source):
+        for h in range(2):
+            src = source.at[:, pl.ds(h * half, half)] if source is block else piece(zp, y, x, h)
+            push(src, piece(zp, y, x, h), asend.at[h, zp], arecv.at[h, zp], across[h])
+        push(source, whole(zp), csend.at[zp], crecv.at[zp], beside)
+
+    def second(zp):
+        for h in range(2):
+            yp, xp = (y, 1 - x) if h == 0 else (1 - y, x)
+            landed(piece(zp, yp, xp, h), arecv.at[h, zp])
+            push(pair(zp, y, x, h), pair(zp, y, x, h), bsend.at[h, zp], brecv.at[h, zp], across[1 - h])
+            push(piece(zp, yp, xp, h), piece(zp, yp, xp, h), cas.at[h, zp], car.at[h, zp], beside)
+
+    def third(zp):
+        for h in range(2):
+            far = pair(zp, 1 - y, 1 - x, h)
+            landed(far, brecv.at[h, zp])
+            push(far, far, cbs.at[h, zp], cbr.at[h, zp], beside)
+
+    def each(k, act):
+        if k == 0:
+            act(z)
+            return
+
+        @pl.when(z >= k)
+        def _():
+            act(z - k)
+
+        @pl.when(z + k < 4)
+        def _():
+            act(z + k)
+
+    own = pltpu.make_async_copy(block, whole(z), local)
+    own.start()
+
+    @pl.when(z < 3)
+    def _():
+        push(block, whole(z), zup.at[z], zrecv.at[z], (me + 4, core))
+
+    @pl.when(z > 0)
+    def _():
+        push(block, whole(z), zdn.at[z], zrecv.at[z], (me - 4, core))
+
+    spread(z, block)
+    own.wait()
+    for k in range(1, 4):
+
+        @pl.when(z >= k)
+        def _():
+            zp = z - k
+            landed(whole(zp), zrecv.at[zp])
+
+            @pl.when(z < 3)
+            def _():
+                push(whole(zp), whole(zp), zup.at[zp], zrecv.at[zp], (me + 4, core))
+
+            spread(zp, whole(zp))
+
+        @pl.when(z + k < 4)
+        def _():
+            zp = z + k
+            landed(whole(zp), zrecv.at[zp])
+
+            @pl.when(z > 0)
+            def _():
+                push(whole(zp), whole(zp), zdn.at[zp], zrecv.at[zp], (me - 4, core))
+
+            spread(zp, whole(zp))
+
+        each(k - 1, second)
+    each(3, second)
+    for k in range(4):
+        each(k, third)
+    other = pl.multiple_of((1 - core) * width, width)
+
+    def theirs(zp, yp, xp, h):
+        return out.at[zp, yp, xp, :, pl.ds(pl.multiple_of(other + h * half, half), half)]
+
+    def theirs_pair(zp, h):
+        span = pl.ds(pl.multiple_of(other + h * half, half), half)
+        if h == 0:
+            return out.at[zp, 1 - y, :, :, span]
+        return out.at[zp, :, 1 - x, :, span]
+
+    for zp in range(4):
+        landed(out.at[zp, y, x, :, pl.ds(other, width)], crecv.at[zp])
+        landed(whole(zp), csend.at[zp])
+        for h in range(2):
+            yp, xp = (y, 1 - x) if h == 0 else (1 - y, x)
+            landed(theirs(zp, yp, xp, h), car.at[h, zp])
+            landed(theirs_pair(zp, h), cbr.at[h, zp])
+            landed(piece(zp, y, x, h), asend.at[h, zp])
+            landed(pair(zp, y, x, h), bsend.at[h, zp])
+            landed(piece(zp, yp, xp, h), cas.at[h, zp])
+            landed(pair(zp, 1 - y, 1 - x, h), cbs.at[h, zp])
+
+        @pl.when((z < 3) & (zp <= z))
+        def _():
+            landed(whole(zp), zup.at[zp])
+
+        @pl.when((z > 0) & (zp >= z))
+        def _():
+            landed(whole(zp), zdn.at[zp])
+
+
+def gather_weight(block):
+    rows, width = block.shape
+    dma = pltpu.SemaphoreType.DMA
+    out = pl.pallas_call(
+        gather_kernel,
+        out_shape=jax.ShapeDtypeStruct((4, 2, 2, rows, 2 * width), block.dtype),
+        in_specs=[pl.BlockSpec(memory_space=pl.ANY)],
+        out_specs=pl.BlockSpec(memory_space=pl.ANY),
+        scratch_shapes=[
+            dma(()),
+            dma((4,)),
+            dma((4,)),
+            dma((4,)),
+            dma((2, 4)),
+            dma((2, 4)),
+            dma((2, 4)),
+            dma((2, 4)),
+            dma((4,)),
+            dma((4,)),
+            dma((2, 4)),
+            dma((2, 4)),
+            dma((2, 4)),
+            dma((2, 4)),
+        ],
+        compiler_params=pltpu.CompilerParams(collective_id=0, has_side_effects=True),
+        cost_estimate=pl.CostEstimate(flops=0, bytes_accessed=100_000_000, transcendentals=0),
+    )(block)
+    return out.reshape(16 * rows, 2 * width)
+
+
+def scatter_kernel(
+    d, out, btake, agive, atake, total, ugive, utake, dgive, dtake,
+    bsend, brecv, asend, arecv, usend, urecv, dsend, drecv,
+):
+    me, core = lax.axis_index("dp"), lax.axis_index("mp")
+    z, y, x = place_of(me)
+    half = d.shape[4] // 2
+    across = ((me + 1 - 2 * x, core), (me + 2 - 4 * y, core))
+    greet(z, y, x, core)
+    first = 3 * (1 - z // 2)
+    third = 1 + z % 2
+    order = (first, 6 - first - third - z, third, z)
+
+    def cols(h):
+        return pl.ds(h * half, half)
+
+    for zp in order:
+        push(d.at[zp, 1 - y, :, :, cols(0)], btake.at[0, zp], bsend.at[0, zp], brecv.at[0, zp], across[1])
+        push(d.at[zp, :, 1 - x, :, cols(1)], btake.at[1, zp], bsend.at[1, zp], brecv.at[1, zp], across[0])
+
+    def wide(value):
+        return value.astype(jnp.float32)
+
+    def middle(zp):
+        for h in range(2):
+            yp, xp, far, near = (y, 1 - x, 1 - x, x) if h == 0 else (1 - y, x, 1 - y, y)
+            landed(btake.at[h, zp], brecv.at[h, zp])
+            agive[h, zp] = (wide(d[zp, yp, xp, :, cols(h)]) + wide(btake[h, zp, far])).astype(d.dtype)
+            push(agive.at[h, zp], atake.at[h, zp], asend.at[h, zp], arecv.at[h, zp], across[h])
+            total[h, zp] = wide(d[zp, y, x, :, cols(h)]) + wide(btake[h, zp, near])
+
+    def line(zp):
+        for h in range(2):
+            landed(atake.at[h, zp], arecv.at[h, zp])
+            total[h, zp] += wide(atake[h, zp])
+
+            @pl.when(zp > z)
+            def _():
+                @pl.when(z > 0)
+                def _():
+                    landed(utake.at[h, zp], urecv.at[h, zp])
+                    total[h, zp] += wide(utake[h, zp])
+
+                ugive[h, zp] = total[h, zp].astype(d.dtype)
+                push(ugive.at[h, zp], utake.at[h, zp], usend.at[h, zp], urecv.at[h, zp], (me + 4, core))
+
+            @pl.when(zp < z)
+            def _():
+                @pl.when(z < 3)
+                def _():
+                    landed(dtake.at[h, zp], drecv.at[h, zp])
+                    total[h, zp] += wide(dtake[h, zp])
+
+                dgive[h, zp] = total[h, zp].astype(d.dtype)
+                push(dgive.at[h, zp], dtake.at[h, zp], dsend.at[h, zp], drecv.at[h, zp], (me - 4, core))
+
+    middle(order[0])
+    for k in range(1, 4):
+        middle(order[k])
+        line(order[k - 1])
+    line(z)
+    for h in range(2):
+
+        @pl.when(z > 0)
+        def _():
+            landed(utake.at[h, z], urecv.at[h, z])
+            total[h, z] += wide(utake[h, z])
+
+        @pl.when(z < 3)
+        def _():
+            landed(dtake.at[h, z], drecv.at[h, z])
+            total[h, z] += wide(dtake[h, z])
+
+        out[:, cols(h)] = total[h, z]
+    for zp in range(4):
+        for h in range(2):
+            landed(btake.at[h, zp], bsend.at[h, zp])
+            landed(atake.at[h, zp], asend.at[h, zp])
+
+            @pl.when(zp > z)
+            def _():
+                landed(ugive.at[h, zp], usend.at[h, zp])
+
+            @pl.when(zp < z)
+            def _():
+                landed(dgive.at[h, zp], dsend.at[h, zp])
+
+
+def scatter_grad(partial):
+    rows, width = partial.shape[0] // 16, partial.shape[1]
+    half = width // 2
+    dma = pltpu.SemaphoreType.DMA
+    one = pltpu.VMEM((2, 4, rows, half), partial.dtype)
+    return pl.pallas_call(
+        scatter_kernel,
+        out_shape=jax.ShapeDtypeStruct((rows, width), jnp.float32),
+        in_specs=[pl.BlockSpec(memory_space=pltpu.VMEM)],
+        out_specs=pl.BlockSpec(memory_space=pltpu.VMEM),
+        scratch_shapes=[
+            pltpu.VMEM((2, 4, 2, rows, half), partial.dtype),
+            one,
+            one,
+            pltpu.VMEM((2, 4, rows, half), jnp.float32),
+            one,
+            one,
+            one,
+            one,
+        ]
+        + [dma((2, 4))] * 8,
+        compiler_params=pltpu.CompilerParams(
+            collective_id=1, has_side_effects=True, vmem_limit_bytes=32 * 1024 * 1024
+        ),
+        cost_estimate=pl.CostEstimate(flops=0, bytes_accessed=100_000_000, transcendentals=0),
+    )(partial.reshape(4, 2, 2, rows, width))
 
 
 def pick(table, index):
@@ -61,8 +385,12 @@
     cores = lax.axis_size("mp")
     me, core = lax.axis_index("dp"), lax.axis_index("mp")
     part, strip = rows // cores, width // cores
-    columns = lax.all_gather(weight, "dp", axis=0, tiled=True)
-    full = lax.all_gather(columns, "mp", axis=1, tiled=True)
+    square = lax.axis_size("dp") == 16 and cores == 2
+    if square:
+        full = gather_weight(weight)
+    else:
+        columns = lax.all_gather(weight, "dp", axis=0, tiled=True)
+        full = lax.all_gather(columns, "mp", axis=1, tiled=True)
     tables = lax.all_gather(destination, "dp", axis=1, tiled=True)
     cot_strip = lax.dynamic_slice_in_dim(cotangent, core * strip, strip, 1)
     cot_all = lax.all_gather(cot_strip, "dp", axis=0, tiled=True)
@@ -85,6 +413,8 @@
     grad_weight = lax.dot_general(
         left_all, right_half, (((0,), (0,)), ((), ())), preferred_element_type=jnp.float32
     ).astype(jnp.bfloat16)
+    if square:
+        return final, grad_in, scatter_grad(grad_weight)
     owned = lax.psum_scatter(grad_weight, "dp", scatter_dimension=0, tiled=True)
     return final, grad_in, owned.astype(jnp.float32)
 

time: 450 us -> 269 us (0.60)
  waiting for transfers between devices: 322 us -> 36.3 us
  Pallas kernels: 0 us -> 105 us
    pallas_call x0 -> x2, Pallas kernels: none -> 105 us  [the longest x1 56.8 us: gather_weight(): pl.pallas_call(gather_kernel, out_shape=jax.ShapeDtypeStruct((4, 2, 2, ro...]
    all_gather x2 -> x0, waiting for transfers between devices: 95.5 us -> none  [the longest x1 80.6 us: body(): columns = lax.all_gather(weight, 'dp', axis=0, tiled=True)]
    reduce_scatter x1 -> x0, waiting for transfers between devices: 89.9 us -> none  [body(): owned = lax.psum_scatter(grad_weight, 'dp', scatter_dimension=0, tiled=True)]
    all_gather x1, waiting for transfers between devices: 65.7 us -> 12.9 us  [body(): last_all = lax.all_gather(last, 'dp', axis=0, tiled=True)]
    all_gather x1, waiting for transfers between devices: 38.1 us -> 0.01 us  [body(): cot_all = lax.all_gather(cot_strip, 'dp', axis=0, tiled=True)]
    psum x1, waiting for transfers between devices: 19.5 us -> 0.02 us  [body(): final = lax.psum(take_rows(slot, last_all), 'mp')]
    all_gather x1, waiting for transfers between devices: 0.02 us -> 8.54 us  [body(): left_all = lax.all_gather(left, 'mp', axis=0, tiled=True)]
  transfers between devices with their start and end apart: 8 -> 5, of which waited for: 7 -> 3; matrix products, arithmetic and copies ran while one was open for 9% -> 23% of each run, Pallas kernels for 0% -> 39%
where the time goes in v2:
time: 269 us
  Pallas kernels  105 us (39%)
  matrix products  55.5 us (21%)
  blocking collectives  44.5 us (17%)
  waiting for transfers between devices  36.3 us (13%)
  between operations  14.1 us (5%)
  local copies, waits for them, and re-layouts  7.4 us (3%)
  other arithmetic  5.29 us (2%)
    pallas_call x1, Pallas kernels, gather_weight(): pl.pallas_call(gather_kernel, out_shape=jax.ShapeDtypeStruct((4, 2, 2, ro...  56.8 us
    pallas_call x1, Pallas kernels, scatter_grad(): pl.pallas_call(scatter_kernel, out_shape=jax.ShapeDtypeStruct((rows, widt...  48.6 us
    all_gather x1, blocking collectives, body(): tables = lax.all_gather(destination, 'dp', axis=1, tiled=True)  39.7 us
    all_gather x1, waiting for transfers between devices, body(): right_all = lax.all_gather(right, 'mp', axis=0, tiled=True)  14.7 us
    dot_general x3, matrix products, recursions(): jnp.dot(grad_branch, weight, preferred_element_type=jnp.float32)  13.5 us
    all_gather x1, waiting for transfers between devices, body(): last_all = lax.all_gather(last, 'dp', axis=0, tiled=True)  12.9 us
    dot_general x3, matrix products, recursions(): lax.dot_general(grad_inner, weight, (((1,), (1,)), ((), ())), preferred_e...  11.7 us
    dot_general x3, matrix products, recursions(): lax.dot_general(gated, weight, (((1,), (1,)), ((), ())), preferred_elemen...  8.95 us
  transfers between devices with their start and end apart: 5, of which 3 were waited for; matrix products, arithmetic and copies ran while one was open for 23% of the time, Pallas kernels for 39%

profile of v2, /device:TPU:0, one launch (start us, length us, event | category | flops | bytes accessed | tf_op | source)
XLA Modules:
  0.0 268.7 jit_solution(5769962607907111521)
XLA Ops:
  7.2 1.0 copy-done
  8.2 0.7 constant_dynamic-slice_fusion
  9.0 0.0 all-gather.5.cloned.1.call-start
  9.0 56.8 %shard_map.76 = bf16[4,2,2,128,2048]{4,3,2,1,0:T(8,128)(2,1)} custom-call(bf16[128,1024]{1,0:T(8,128)(2,1)} %block.1), custom_call_target="tpu_custom_call" | custom-call | bytes 100000000 | tf_op jit(solution)/shard_map/pallas_call | solution.py:188
  65.9 0.2 fusion.28
  66.1 0.1 compare_convert_fusion
  66.2 5.2 %fusion.39 = f32[64,2048]{1,0:T(8,128)S(1)} fusion(bf16[2048,2048]{1,0:T(8,128)(2,1)} %bitcast.26, f32[64]{0:T(128)S(1)} %add_rsqrt_fusion.2, bf16[128,2048]{1,0:T(8,128)(2,1)S(1)} %copy-done.1, s32[]{:T(128)S(6)} %select_n.77), kind=kOutput, calls=%fused_computation.75 | convolution fusion | flops 537264128 | bytes 9175556 | tf_op jit(solution)/shard_map/dot_general | solution.py:354
  71.3 1.0 slice-done.1
  72.3 2.8 %multiply_reduce_fusion.3 = (f32[64]{0:T(128)S(1)}, f32[64,2048]{1,0:T(8,128)S(1)}) fusion(bf16[2048,2048]{1,0:T(8,128)(2,1)S(1)} %bitcast.32, f32[64,2048]{1,0:T(8,128)S(1)} %fusion.39, f32[64]{0:T(128)S(1)} %get-tuple-element.14, bf16[128,2048]{1,0:T(8,128)(2,1)S(1)} %copy-done.1, s32[]{:T(128)S(6)} %select_n.77), kind=kOutput, calls=%fused_computation.64 | convolution fusion | flops 538443712 | bytes 9699844 | tf_op jit(solution)/shard_map/dot_general | solution.py:356
  75.1 1.7 fusion.45
  76.8 2.8 %multiply_reduce_fusion.2 = (f32[64]{0:T(128)S(1)}, f32[64,2048]{1,0:T(8,128)S(1)}) fusion(f32[64,2048]{1,0:T(8,128)S(1)} %get-tuple-element.16, bf16[2048,2048]{1,0:T(8,128)(2,1)S(1)} %bitcast.34, f32[64,2048]{1,0:T(8,128)S(1)} %fusion.45, f32[64]{0:T(128)S(1)} %get-tuple-element.13), kind=kOutput, calls=%fused_computation.61 | convolution fusion | flops 538312640 | bytes 9961984 | tf_op jit(solution)/shard_map/dot_general | solution.py:356
  79.6 1.7 fusion.46
  81.3 3.4 %fusion.10 = bf16[64,2048]{1,0:T(8,128)(2,1)} fusion(f32[64,2048]{1,0:T(8,128)S(1)} %get-tuple-element.18, bf16[2048,2048]{1,0:T(8,128)(2,1)S(1)} %bitcast.36, f32[64]{0:T(128)S(1)} %get-tuple-element.12, f32[64,2048]{1,0:T(8,128)S(1)} %fusion.46), kind=kOutput, calls=%fused_computation.18 | convolution fusion | flops 537919488 | bytes 9699584 | tf_op jit(solution)/shard_map/dot_general | solution.py:356
  84.7 0.0 all-gather.9.cloned.1.call-start
  84.7 39.7 %all_gather.21 = s32[3,2048]{1,0:T(4,128)S(1)} all-gather(s32[3,128]{1,0:T(4,128)S(1)} %copy-done.6), channel_id=1, replica_groups=mesh['dp'=16,'mp'=2] {'dp'}, dimensions={1}, use_global_device_ids=true | all-gather | bytes 26112 | tf_op jit(solution)/shard_map/all_gather | solution.py:394
  124.5 0.3 select_reduce_fusion.1
  124.8 0.4 select_reduce_fusion
  125.2 0.8 constant_dynamic-update-slice_fusion.1
  126.0 3.3 %convolution_convert_fusion.2 = bf16[128,1024]{1,0:T(8,128)(2,1)S(1)} fusion(bf16[2048,1024]{1,0:T(8,128)(2,1)} %all-gather.7.cloned.1.call-done, s32[128]{0:T(128)S(1)} %get-tuple-element.3), kind=kOutput, calls=%fused_computation.23 | convolution fusion | flops 537264128 | bytes 4456960 | tf_op jit(solution)/shard_map/dot_general | solution.py:343
  129.3 2.4 all_gather.24
  131.7 5.3 %constant_dynamic-update-slice_fusion.7 = (bf16[384,2048]{1,0:T(8,128)(2,1)S(1)}, bf16[64,2048]{1,0:T(8,128)(2,1)S(1)}) fusion(f32[64,2048]{1,0:T(8,128)S(1)} %fusion.46, bf16[2048,2048]{1,0:T(8,128)(2,1)} %bitcast.27, f32[64]{0:T(128)S(1)} %get-tuple-element.12, bf16[128,2048]{1,0:T(8,128)(2,1)S(1)} %all_gather.24, s32[]{:T(128)S(6)} %select_n.77), kind=kOutput, calls=%fused_computation.83 | convolution fusion | flops 538443776 | bytes 9699844 | tf_op jit(solution)/shard_map/dot_general | solution.py:368
  137.0 2.8 %multiply_reduce_fusion.1 = (f32[64]{0:T(128)S(1)}, f32[64,2048]{1,0:T(8,128)S(1)}) fusion(f32[64,2048]{1,0:T(8,128)S(1)} %get-tuple-element.18, bf16[64,2048]{1,0:T(8,128)(2,1)S(1)} %get-tuple-element.26, bf16[2048,2048]{1,0:T(8,128)(2,1)S(1)} %bitcast.39), kind=kOutput, calls=%fused_computation.57 | convolution fusion | flops 537132992 | bytes 9699584 | tf_op jit(solution)/shard_map/dot_general | solution.py:371
  139.8 0.1 fusion.36
  139.9 0.1 constant_dynamic-update-slice_fusion.6
  140.1 0.1 constant_dynamic-update-slice_fusion
  140.2 0.3 fusion.34
  140.4 1.8 constant_dynamic-update-slice_fusion.5
  142.2 2.8 %multiply_reduce_fusion = (f32[64]{0:T(128)S(1)}, f32[64,2048]{1,0:T(8,128)S(1)}) fusion(f32[64,2048]{1,0:T(8,128)S(1)} %get-tuple-element.16, bf16[64,2048]{1,0:T(8,128)(2,1)S(1)} %get-tuple-element.28, bf16[2048,2048]{1,0:T(8,128)(2,1)S(1)} %bitcast.41), kind=kOutput, calls=%fused_computation.56 | convolution fusion | flops 537132992 | bytes 9699584 | tf_op jit(solution)/shard_map/dot_general | solution.py:371
  145.0 0.1 fusion.38
  145.2 0.3 fusion.32
  145.4 1.1 copy-done.5
  146.7 0.9 constant_dynamic-update-slice_fusion.4
  147.5 6.4 %constant_dynamic-update-slice_fusion.3 = (bf16[384,2048]{1,0:T(8,128)(2,1)}, bf16[64,2048]{1,0:T(8,128)(2,1)S(1)}) fusion(bf16[384,2048]{1,0:T(8,128)(2,1)} %constant_dynamic-update-slice_fusion.4, f32[64,2048]{1,0:T(8,128)S(1)} %fusion.39, bf16[2048,2048]{1,0:T(8,128)(2,1)} %bitcast.28, bf16[64,2048]{1,0:T(8,128)(2,1)S(1)} %get-tuple-element.6, ...), kind=kOutput, calls=%fused_computation.79 | convolution fusion | flops 538443776 | bytes 9699584 | tf_op jit(solution)/shard_map/dot_general | solution.py:368
  153.9 0.8 constant_dynamic-update-slice_fusion.2
  154.8 0.3 select_reduce_fusion.3
  155.1 0.3 select_reduce_fusion.2
  155.4 6.2 %fusion.29 = (f32[64]{0:T(128)S(1)}, f32[64,2048]{1,0:T(8,128)S(1)}) fusion(bf16[128,2048]{1,0:T(8,128)(2,1)S(1)} %copy-done.2, s32[]{:T(128)S(6)} %select_n.77, bf16[64,2048]{1,0:T(8,128)(2,1)S(1)} %get-tuple-element.30, bf16[2048,2048]{1,0:T(8,128)(2,1)} %bitcast.29), kind=kOutput, calls=%fused_computation.55 | convolution fusion | flops 537264064 | bytes 9437444 | tf_op jit(solution)/shard_map/dot_general | solution.py:371
  161.6 0.2 fusion.20
  161.9 2.4 all_gather.25
  164.3 12.9 %all-gather.5.cloned.1.call-done = bf16[1024,2048]{1,0:T(8,128)(2,1)} async-done(((bf16[64,2048]{1,0:T(8,128)(2,1)}), bf16[1024,2048]{1,0:T(8,128)(2,1)}) %all-gather.5.cloned.1.call-update) | async-done | bytes 4194320 | tf_op jit(solution)/shard_map/all_gather | solution.py:405
  177.2 3.7 %convolution_convert_fusion.1 = bf16[128,2048]{1,0:T(8,128)(2,1)} fusion(bf16[1024,2048]{1,0:T(8,128)(2,1)} %all-gather.5.cloned.1.call-done, s32[128]{0:T(128)S(1)} %compare_select_fusion), kind=kOutput, calls=%fused_computation.1 | convolution fusion | flops 537264128 | bytes 4719104 | tf_op jit(solution)/shard_map/dot_general | solution.py:343
  181.0 8.5 %all-gather.9.cloned.1.call-done = bf16[768,2048]{1,0:T(8,128)(2,1)} async-done(((bf16[384,2048]{1,0:T(8,128)(2,1)}), bf16[768,2048]{1,0:T(8,128)(2,1)}) %all-gather.9.cloned.1.call-update) | async-done | bytes 3145744 | tf_op jit(solution)/shard_map/all_gather | solution.py:410
  189.5 14.7 %all-gather.11.cloned.1.call-done = bf16[768,2048]{1,0:T(8,128)(2,1)} async-done(((bf16[384,2048]{1,0:T(8,128)(2,1)}), bf16[768,2048]{1,0:T(8,128)(2,1)}) %all-gather.11.cloned.1.call-update) | async-done | bytes 3145744 | tf_op jit(solution)/shard_map/all_gather | solution.py:411
  204.2 5.8 %convolution_convert_fusion = bf16[2048,1024]{1,0:T(8,128)(2,1)S(1)} fusion(bf16[768,2048]{1,0:T(8,128)(2,1)} %all-gather.9.cloned.1.call-done, bf16[768,2048]{1,0:T(8,128)(2,1)} %all-gather.11.cloned.1.call-done, s32[]{:T(128)S(6)} %select_n.80), kind=kOutput, calls=%fused_computation | convolution fusion | flops 3223322624 | bytes 8912900 | tf_op jit(solution)/shard_map/dot_general | solution.py:413
  210.1 48.6 %shard_map.77 = f32[128,1024]{1,0:T(8,128)S(1)} custom-call(bf16[4,2,2,128,1024]{4,3,2,1,0:T(8,128)(2,1)S(1)} %bitcast.25), custom_call_target="tpu_custom_call" | custom-call | bytes 100000000 | tf_op jit(solution)/shard_map/pallas_call | solution.py:308
  258.7 1.9 copy.21
  260.6 0.8 copy.22
  261.4 0.8 copy.23
  (43 shorter events, 0.4 us)
Async XLA Ops:
  7.2 1.0 copy-start
  7.2 118.8 %all-gather.7.cloned.1.call-start = ((), (), s32[]{:S(2)}) async-start(), calls=%async_computation.2 | async-start | bytes 4456448 | tf_op jit(solution)/shard_map/all_gather | solution.py:396
  9.0 168.2 %all-gather.5.cloned.1.call-start = ((), (), s32[]{:S(2)}) async-start(), calls=%async_computation | async-start | bytes 4456448 | tf_op jit(solution)/shard_map/all_gather | solution.py:405
  9.0 56.9 %copy-start.1 = (bf16[128,2048]{1,0:T(8,128)(2,1)S(1)}, bf16[128,2048]{1,0:T(8,128)(2,1)}, u32[]{:S(2)}) copy-start(bf16[128,2048]{1,0:T(8,128)(2,1)} %param.5) | copy-start | bytes 1572868
  9.0 57.0 %copy-start.7 = (s32[128]{0:T(128)S(1)}, s32[128]{0:T(128)}, u32[]{:S(2)}) copy-start(s32[128]{0:T(128)} %param.6) | copy-start | bytes 1540
  65.9 5.4 %slice-start = ((s8[8388608]{0:T(1024)(128)(4,1)}), s8[4194304]{0:T(1024)(128)(4,1)S(1)}, s32[]{:S(2)}) async-start(s8[8388608]{0:T(1024)(128)(4,1)} %bitcast.30), calls=%async_computation.5 | async-start | bytes 8388608
  66.2 6.2 %slice-start.1 = ((s8[8388608]{0:T(1024)(128)(4,1)}), s8[4194304]{0:T(1024)(128)(4,1)S(1)}, s32[]{:S(2)}) async-start(s8[8388608]{0:T(1024)(128)(4,1)} %bitcast.30), calls=%async_computation.6 | async-start | bytes 8388608
  81.3 3.5 %copy-start.6 = (s32[3,128]{1,0:T(4,128)S(1)}, s32[3,128]{1,0:T(4,128)}, u32[]{:S(2)}) copy-start(s32[3,128]{1,0:T(4,128)} %param.7) | copy-start | bytes 4612
  84.7 104.8 %all-gather.9.cloned.1.call-start = ((), (), s32[]{:S(2)}) async-start(), calls=%async_computation.3 | async-start | bytes 4718592 | tf_op jit(solution)/shard_map/all_gather | solution.py:410
  126.0 11.0 %slice-start.2 = ((s8[8388608]{0:T(1024)(128)(4,1)}), s8[4194304]{0:T(1024)(128)(4,1)S(1)}, s32[]{:S(2)}) async-start(s8[8388608]{0:T(1024)(128)(4,1)} %bitcast.37), calls=%async_computation.7 | async-start | bytes 8388608
  131.7 5.3 %slice-start.3 = ((s8[8388608]{0:T(1024)(128)(4,1)}), s8[4194304]{0:T(1024)(128)(4,1)S(1)}, s32[]{:S(2)}) async-start(s8[8388608]{0:T(1024)(128)(4,1)} %bitcast.37), calls=%async_computation.8 | async-start | bytes 8388608
  137.0 2.8 %copy-start.4 = (bf16[384,2048]{1,0:T(8,128)(2,1)S(1)}, bf16[384,2048]{1,0:T(8,128)(2,1)}, u32[]{:S(2)}) copy-start(bf16[384,2048]{1,0:T(8,128)(2,1)} %constant_dynamic-update-slice_fusion.1) | copy-start | bytes 4718596
  142.2 2.8 %copy-start.3 = (bf16[384,2048]{1,0:T(8,128)(2,1)}, bf16[384,2048]{1,0:T(8,128)(2,1)S(1)}, u32[]{:S(2)}) copy-start(bf16[384,2048]{1,0:T(8,128)(2,1)S(1)} %get-tuple-element.27) | copy-start | bytes 4718596
  142.2 2.8 %copy-start.2 = (bf16[128,2048]{1,0:T(8,128)(2,1)S(1)}, bf16[128,2048]{1,0:T(8,128)(2,1)}, u32[]{:S(2)}) copy-start(bf16[128,2048]{1,0:T(8,128)(2,1)} %param.5) | copy-start | bytes 1572868
  145.4 1.2 copy-start.5
  146.6 57.6 %all-gather.11.cloned.1.call-start = ((), (), s32[]{:S(2)}) async-start(), calls=%async_computation.4 | async-start | bytes 4718592 | tf_op jit(solution)/shard_map/all_gather | solution.py:411
  154.8 103.9 %all-reduce.2.cloned.1.call-start = ((), (), s32[]{:S(2)}) async-start(), calls=%async_computation.1 | async-start | bytes 1048576 | tf_op jit(solution)/shard_map/psum | solution.py:408
Sparse Core Ops, SparseCore 0:
  11.4 88.0 all-gather.6
  102.8 74.3 all-gather.4
  178.7 10.7 all-gather.8
  190.9 13.2 all-gather.10
  207.0 19.8 all-reduce.1

commit v3 on v2

--- a/solution.py
+++ b/solution.py
@@ -7,6 +7,7 @@
 
 
 MESH = pl.DeviceIdType.MESH
+TILE = 512
 
 
 def push(src, dst, send, recv, device):
@@ -51,52 +52,75 @@
     pl.semaphore_wait(barrier, 3 + (1 - z // 3) + (z + 2) // 3)
 
 
-def gather_kernel(
-    block, out, local, zup, zdn, zrecv, asend, arecv, bsend, brecv, csend, crecv, cas, car, cbs, cbr
-):
-    me, core = lax.axis_index("dp"), lax.axis_index("mp")
-    z, y, x = place_of(me)
-    width = block.shape[1]
-    half = width // 2
-    base = pl.multiple_of(core * width, width)
-    beside = (me, 1 - core)
-    across = ((me + 1 - 2 * x, core), (me + 2 - 4 * y, core))
-    greet(z, y, x, core)
-
-    def cols(h):
-        return pl.ds(pl.multiple_of(core * width + h * half, half), half)
-
-    def whole(zp):
-        return out.at[zp, y, x, :, pl.ds(base, width)]
-
-    def piece(zp, yp, xp, h):
-        return out.at[zp, yp, xp, :, cols(h)]
-
-    def pair(zp, yp, xp, h):
+class Relay:
+    def __init__(self, block, out, sems, paths=(0, 1), beside=False):
+        self.block, self.out, self.sems, self.paths, self.beside = block, out, sems, paths, beside
+        self.me, self.core = lax.axis_index("dp"), lax.axis_index("mp")
+        self.z, self.y, self.x = place_of(self.me)
+        self.width = block.shape[1]
+        self.half = self.width // len(paths)
+        self.sibling = (self.me, 1 - self.core)
+        me, x, y = self.me, self.x, self.y
+        self.across = ((me + 1 - 2 * x, self.core), (me + 2 - 4 * y, self.core))
+
+    def span(self, h, core=None):
+        core = self.core if core is None else core
+        if not self.beside:
+            return pl.ds(h * self.half, self.half)
+        return pl.ds(pl.multiple_of(core * self.width + h * self.half, self.half), self.half)
+
+    def whole(self, zp, core=None):
+        core = self.core if core is None else core
+        if not self.beside:
+            return self.out.at[zp, self.y, self.x]
+        start = pl.multiple_of(core * self.width, self.width)
+        return self.out.at[zp, self.y, self.x, :, pl.ds(start, self.width)]
+
+    def piece(self, zp, far, h, core=None):
+        x, y = self.x, self.y
+        if far:
+            x, y = (1 - x, y) if h == 0 else (x, 1 - y)
+        return self.out.at[zp, y, x, :, self.span(h, core)]
+
+    def pair(self, zp, far, h, core=None):
         if h == 0:
-            return out.at[zp, yp, :, :, cols(0)]
-        return out.at[zp, :, xp, :, cols(1)]
-
-    def spread(zp, source):
-        for h in range(2):
-            src = source.at[:, pl.ds(h * half, half)] if source is block else piece(zp, y, x, h)
-            push(src, piece(zp, y, x, h), asend.at[h, zp], arecv.at[h, zp], across[h])
-        push(source, whole(zp), csend.at[zp], crecv.at[zp], beside)
-
-    def second(zp):
-        for h in range(2):
-            yp, xp = (y, 1 - x) if h == 0 else (1 - y, x)
-            landed(piece(zp, yp, xp, h), arecv.at[h, zp])
-            push(pair(zp, y, x, h), pair(zp, y, x, h), bsend.at[h, zp], brecv.at[h, zp], across[1 - h])
-            push(piece(zp, yp, xp, h), piece(zp, yp, xp, h), cas.at[h, zp], car.at[h, zp], beside)
-
-    def third(zp):
-        for h in range(2):
-            far = pair(zp, 1 - y, 1 - x, h)
-            landed(far, brecv.at[h, zp])
-            push(far, far, cbs.at[h, zp], cbr.at[h, zp], beside)
-
-    def each(k, act):
+            y = 1 - self.y if far else self.y
+            return self.out.at[zp, y, :, :, self.span(0, core)]
+        x = 1 - self.x if far else self.x
+        return self.out.at[zp, :, x, :, self.span(1, core)]
+
+    def spread(self, zp, own):
+        asend, arecv = self.sems[4:6]
+        for h in self.paths:
+            src = self.piece(zp, False, h)
+            if own:
+                src = self.block.at[:, pl.ds(h * self.half, self.half)]
+            push(src, self.piece(zp, False, h), asend.at[h, zp], arecv.at[h, zp], self.across[h])
+        if self.beside:
+            csend, crecv = self.sems[8:10]
+            src = self.block if own else self.whole(zp)
+            push(src, self.whole(zp), csend.at[zp], crecv.at[zp], self.sibling)
+
+    def second(self, zp):
+        arecv, bsend, brecv = self.sems[5:8]
+        for h in self.paths:
+            got, both = self.piece(zp, True, h), self.pair(zp, False, h)
+            landed(got, arecv.at[h, zp])
+            push(both, both, bsend.at[h, zp], brecv.at[h, zp], self.across[1 - h])
+            if self.beside:
+                cas, car = self.sems[10:12]
+                push(got, got, cas.at[h, zp], car.at[h, zp], self.sibling)
+
+    def third(self, zp):
+        for h in self.paths:
+            got = self.pair(zp, True, h)
+            landed(got, self.sems[7].at[h, zp])
+            if self.beside:
+                cbs, cbr = self.sems[12:14]
+                push(got, got, cbs.at[h, zp], cbr.at[h, zp], self.sibling)
+
+    def each(self, k, act):
+        z = self.z
         if k == 0:
             act(z)
             return
@@ -109,107 +133,260 @@
         def _():
             act(z + k)
 
-    own = pltpu.make_async_copy(block, whole(z), local)
-    own.start()
-
-    @pl.when(z < 3)
-    def _():
-        push(block, whole(z), zup.at[z], zrecv.at[z], (me + 4, core))
-
-    @pl.when(z > 0)
-    def _():
-        push(block, whole(z), zdn.at[z], zrecv.at[z], (me - 4, core))
-
-    spread(z, block)
-    own.wait()
+    def up(self, zp, src):
+        zup, zrecv = self.sems[1], self.sems[3]
+
+        @pl.when(self.z < 3)
+        def _():
+            push(src, self.whole(zp), zup.at[zp], zrecv.at[zp], (self.me + 4, self.core))
+
+    def down(self, zp, src):
+        zdn, zrecv = self.sems[2], self.sems[3]
+
+        @pl.when(self.z > 0)
+        def _():
+            push(src, self.whole(zp), zdn.at[zp], zrecv.at[zp], (self.me - 4, self.core))
+
+    def start(self):
+        z = self.z
+        own = pltpu.make_async_copy(self.block, self.whole(z), self.sems[0])
+        own.start()
+        self.up(z, self.block)
+        self.down(z, self.block)
+        self.spread(z, True)
+        own.wait()
+
+    def step(self, k):
+        z = self.z
+
+        @pl.when(z >= k)
+        def _():
+            zp = z - k
+            landed(self.whole(zp), self.sems[3].at[zp])
+            self.up(zp, self.whole(zp))
+            self.spread(zp, False)
+
+        @pl.when(z + k < 4)
+        def _():
+            zp = z + k
+            landed(self.whole(zp), self.sems[3].at[zp])
+            self.down(zp, self.whole(zp))
+            self.spread(zp, False)
+
+        self.each(k - 1, self.second)
+
+    def finish(self):
+        self.each(3, self.second)
+        for k in range(4):
+            self.each(k, self.third)
+        z, other = self.z, 1 - self.core
+        for zp in range(4):
+            for h in self.paths:
+                landed(self.piece(zp, False, h), self.sems[4].at[h, zp])
+                landed(self.pair(zp, False, h), self.sems[6].at[h, zp])
+            if self.beside:
+                csend, crecv, cas, car, cbs, cbr = self.sems[8:14]
+                landed(self.whole(zp, other), crecv.at[zp])
+                landed(self.whole(zp), csend.at[zp])
+                for h in self.paths:
+                    landed(self.piece(zp, True, h, other), car.at[h, zp])
+                    landed(self.pair(zp, True, h, other), cbr.at[h, zp])
+                    landed(self.piece(zp, True, h), cas.at[h, zp])
+                    landed(self.pair(zp, True, h), cbs.at[h, zp])
+
+            @pl.when((z < 3) & (zp <= z))
+            def _():
+                landed(self.whole(zp), self.sems[1].at[zp])
+
+            @pl.when((z > 0) & (zp >= z))
+            def _():
+                landed(self.whole(zp), self.sems[2].at[zp])
+
+
+def relay_sems(beside):
+    dma = pltpu.SemaphoreType.DMA
+    base = [dma(()), dma((4,)), dma((4,)), dma((4,))] + [dma((2, 4))] * 4
+    return base + ([dma((4,)), dma((4,))] + [dma((2, 4))] * 4 if beside else [])
+
+
+def enter():
+    me, core = lax.axis_index("dp"), lax.axis_index("mp")
+    greet(*place_of(me), core)
+
+
+def gather_kernel(block, table, out, tables, *sems):
+    main = Relay(block, out, sems[:14], beside=True)
+    small = Relay(table, tables, sems[14:], paths=(0,))
+    enter()
+    main.start()
+    small.start()
     for k in range(1, 4):
-
-        @pl.when(z >= k)
-        def _():
-            zp = z - k
-            landed(whole(zp), zrecv.at[zp])
-
-            @pl.when(z < 3)
-            def _():
-                push(whole(zp), whole(zp), zup.at[zp], zrecv.at[zp], (me + 4, core))
-
-            spread(zp, whole(zp))
-
-        @pl.when(z + k < 4)
-        def _():
-            zp = z + k
-            landed(whole(zp), zrecv.at[zp])
-
-            @pl.when(z > 0)
-            def _():
-                push(whole(zp), whole(zp), zdn.at[zp], zrecv.at[zp], (me - 4, core))
-
-            spread(zp, whole(zp))
-
-        each(k - 1, second)
-    each(3, second)
-    for k in range(4):
-        each(k, third)
-    other = pl.multiple_of((1 - core) * width, width)
-
-    def theirs(zp, yp, xp, h):
-        return out.at[zp, yp, xp, :, pl.ds(pl.multiple_of(other + h * half, half), half)]
-
-    def theirs_pair(zp, h):
-        span = pl.ds(pl.multiple_of(other + h * half, half), half)
-        if h == 0:
-            return out.at[zp, 1 - y, :, :, span]
-        return out.at[zp, :, 1 - x, :, span]
-
-    for zp in range(4):
-        landed(out.at[zp, y, x, :, pl.ds(other, width)], crecv.at[zp])
-        landed(whole(zp), csend.at[zp])
-        for h in range(2):
-            yp, xp = (y, 1 - x) if h == 0 else (1 - y, x)
-            landed(theirs(zp, yp, xp, h), car.at[h, zp])
-            landed(theirs_pair(zp, h), cbr.at[h, zp])
-            landed(piece(zp, y, x, h), asend.at[h, zp])
-            landed(pair(zp, y, x, h), bsend.at[h, zp])
-            landed(piece(zp, yp, xp, h), cas.at[h, zp])
-            landed(pair(zp, 1 - y, 1 - x, h), cbs.at[h, zp])
-
-        @pl.when((z < 3) & (zp <= z))
-        def _():
-            landed(whole(zp), zup.at[zp])
-
-        @pl.when((z > 0) & (zp >= z))
-        def _():
-            landed(whole(zp), zdn.at[zp])
-
-
-def gather_weight(block):
+        main.step(k)
+        small.step(k)
+    small.finish()
+    main.finish()
+
+
+def params(number):
+    return pltpu.CompilerParams(
+        collective_id=number, has_side_effects=True, vmem_limit_bytes=48 * 1024 * 1024
+    )
+
+
+def gather_weight(block, table):
     rows, width = block.shape
+    anywhere = pl.BlockSpec(memory_space=pl.ANY)
+    out, tables = pl.pallas_call(
+        gather_kernel,
+        out_shape=(
+            jax.ShapeDtypeStruct((4, 2, 2, rows, 2 * width), block.dtype),
+            jax.ShapeDtypeStruct((4, 2, 2) + table.shape, table.dtype),
+        ),
+        in_specs=[anywhere, anywhere],
+        out_specs=(anywhere, anywhere),
+        scratch_shapes=relay_sems(True) + relay_sems(False),
+        compiler_params=params(0),
+        cost_estimate=pl.CostEstimate(flops=0, bytes_accessed=100_000_000, transcendentals=0),
+    )(block, table)
+    tables = tables.reshape((16,) + table.shape).transpose(1, 0, 2).reshape(table.shape[0], -1)
+    return out.reshape(16 * rows, 2 * width), tables
+
+
+def times(left, weight, out):
+    @pl.loop(0, weight.shape[1] // TILE)
+    def _(j):
+        span = pl.ds(pl.multiple_of(j * TILE, TILE), TILE)
+        out[:, span] = jnp.dot(left[...], weight[:, span], preferred_element_type=jnp.float32)
+
+
+def times_transposed(left, weight, out):
+    @pl.loop(0, weight.shape[0] // TILE)
+    def _(j):
+        span = pl.ds(pl.multiple_of(j * TILE, TILE), TILE)
+        out[:, span] = lax.dot_general(
+            left[...], weight[span, :], (((1,), (1,)), ((), ())), preferred_element_type=jnp.float32
+        )
+
+
+def scale_of(state_f):
+    return lax.rsqrt(jnp.mean(state_f * state_f, axis=-1, keepdims=True) + 1e-06)
+
+
+def forward_kernel(state, levels, weight, block, xs, us, last, out, low, wide, *sems):
+    relay = Relay(block, out, sems)
+    enter()
+    relay.start()
+    last[...] = state[...]
+    for step in range(3):
+        xs[step] = last[...]
+        state_f = last[...].astype(jnp.float32)
+        low[...] = (state_f * scale_of(state_f)).astype(jnp.bfloat16)
+        times(low, weight, us.at[step])
+        inner = us[step]
+        low[...] = (inner / (1.0 + jnp.exp(-inner))).astype(jnp.bfloat16)
+        times_transposed(low, weight, wide)
+        active = (levels[...] >= step + 1).astype(jnp.float32)
+        last[...] = (last[...].astype(jnp.float32) + active * wide[...]).astype(jnp.bfloat16)
+        relay.step(step + 1)
+    relay.finish()
+
+
+def forward(state, levels, weight, block):
+    rows, width = state.shape
+    vmem, anywhere = pl.BlockSpec(memory_space=pltpu.VMEM), pl.BlockSpec(memory_space=pl.ANY)
+    xs, us, last, out = pl.pallas_call(
+        forward_kernel,
+        out_shape=(
+            jax.ShapeDtypeStruct((3, rows, width), jnp.bfloat16),
+            jax.ShapeDtypeStruct((3, rows, width), jnp.float32),
+            jax.ShapeDtypeStruct((rows, width), jnp.bfloat16),
+            jax.ShapeDtypeStruct((4, 2, 2) + block.shape, block.dtype),
+        ),
+        in_specs=[vmem, vmem, vmem, anywhere],
+        out_specs=(vmem, vmem, vmem, anywhere),
+        scratch_shapes=[
+            pltpu.VMEM((rows, width), jnp.bfloat16),
+            pltpu.VMEM((rows, width), jnp.float32),
+        ]
+        + relay_sems(False),
+        compiler_params=params(2),
+    )(state, levels, weight, block)
+    return xs, us, last, out.reshape(16 * block.shape[0], block.shape[1])
+
+
+def backward_kernel(
+    xs, us, levels, cot, weight, block, grad, lefts, rights, out,
+    full, wide, dx, lsend, lrecv, rsend, rrecv, *sems
+):
+    relay = Relay(block, out, sems)
+    core, sibling = relay.core, relay.sibling
+    half = rights.shape[3]
+    mine = pl.ds(pl.multiple_of(core * half, half), half)
+    theirs = pl.ds(pl.multiple_of((1 - core) * half, half), half)
+    enter()
+    relay.start()
+    dx[...] = cot[...].astype(jnp.float32)
+
+    def share(i):
+        push(lefts.at[core, i], lefts.at[core, i], lsend.at[i], lrecv.at[i], sibling)
+        rights[core, i] = full[i, :, mine]
+        push(full.at[i, :, theirs], rights.at[core, i], rsend.at[i], rrecv.at[i], sibling)
+
+    for turn, step in enumerate((2, 1, 0)):
+        a, b = 2 * step, 2 * step + 1
+        state_f = xs[step].astype(jnp.float32)
+        rinv = scale_of(state_f)
+        lefts[core, a] = (state_f * rinv).astype(jnp.bfloat16)
+        active = (levels[...] >= step + 1).astype(jnp.float32)
+        lefts[core, b] = (active * dx[...]).astype(jnp.bfloat16)
+        times(lefts.at[core, b], weight, wide)
+        inner = us[step]
+        sigma = 1.0 / (1.0 + jnp.exp(-inner))
+        full[b] = (inner * sigma).astype(jnp.bfloat16)
+        full[a] = (wide[...] * sigma * (1.0 + inner * (1.0 - sigma))).astype(jnp.bfloat16)
+        share(a)
+        share(b)
+        times_transposed(full.at[a], weight, wide)
+        state_f = xs[step].astype(jnp.float32)
+        mean = jnp.mean(wide[...] * state_f, axis=-1, keepdims=True)
+        entry = dx[...] + rinv * wide[...] - state_f * (rinv * rinv * rinv * mean)
+        dx[...] = entry.astype(jnp.bfloat16).astype(jnp.float32)
+        relay.step(turn + 1)
+    grad[...] = dx[...].astype(jnp.bfloat16)
+    for i in range(6):
+        landed(lefts.at[1 - core, i], lrecv.at[i])
+        landed(rights.at[1 - core, i], rrecv.at[i])
+        landed(lefts.at[core, i], lsend.at[i])
+        landed(full.at[i, :, theirs], rsend.at[i])
+    relay.finish()
+
+
+def backward(xs, us, levels, cot, weight, block):
+    rows, width = cot.shape
+    half = weight.shape[1] // 2
+    vmem, anywhere = pl.BlockSpec(memory_space=pltpu.VMEM), pl.BlockSpec(memory_space=pl.ANY)
     dma = pltpu.SemaphoreType.DMA
-    out = pl.pallas_call(
-        gather_kernel,
-        out_shape=jax.ShapeDtypeStruct((4, 2, 2, rows, 2 * width), block.dtype),
-        in_specs=[pl.BlockSpec(memory_space=pl.ANY)],
-        out_specs=pl.BlockSpec(memory_space=pl.ANY),
+    grad, lefts, rights, out = pl.pallas_call(
+        backward_kernel,
+        out_shape=(
+            jax.ShapeDtypeStruct((rows, width), jnp.bfloat16),
+            jax.ShapeDtypeStruct((2, 6, rows, width), jnp.bfloat16),
+            jax.ShapeDtypeStruct((2, 6, rows, half), jnp.bfloat16),
+            jax.ShapeDtypeStruct((4, 2, 2) + block.shape, block.dtype),
+        ),
+        in_specs=[vmem] * 5 + [anywhere],
+        out_specs=(vmem, vmem, vmem, anywhere),
         scratch_shapes=[
-            dma(()),
-            dma((4,)),
-            dma((4,)),
-            dma((4,)),
-            dma((2, 4)),
-            dma((2, 4)),
-            dma((2, 4)),
-            dma((2, 4)),
-            dma((4,)),
-            dma((4,)),
-            dma((2, 4)),
-            dma((2, 4)),
-            dma((2, 4)),
-            dma((2, 4)),
-        ],
-        compiler_params=pltpu.CompilerParams(collective_id=0, has_side_effects=True),
-        cost_estimate=pl.CostEstimate(flops=0, bytes_accessed=100_000_000, transcendentals=0),
-    )(block)
-    return out.reshape(16 * rows, 2 * width)
+            pltpu.VMEM((6, rows, 2 * half), jnp.bfloat16),
+            pltpu.VMEM((rows, width), jnp.float32),
+            pltpu.VMEM((rows, width), jnp.float32),
+        ]
+        + [dma((6,))] * 4
+        + relay_sems(False),
+        compiler_params=params(3),
+    )(xs, us, levels, cot, weight, block)
+    merged = out.reshape(16 * block.shape[0], block.shape[1])
+    return grad, lefts.reshape(-1, width), rights.reshape(-1, half), merged
 
 
 def scatter_kernel(
@@ -386,30 +563,35 @@
     me, core = lax.axis_index("dp"), lax.axis_index("mp")
     part, strip = rows // cores, width // cores
     square = lax.axis_size("dp") == 16 and cores == 2
+    state = lax.dynamic_slice_in_dim(hidden_in, core * part, part, 0)
+    levels = lax.dynamic_slice_in_dim(depth, core * part, part, 0)
+    cot_strip = lax.dynamic_slice_in_dim(cotangent, core * strip, strip, 1)
     if square:
-        full = gather_weight(weight)
+        full, tables = gather_weight(weight, destination)
+        high = levels.astype(jnp.float32)[:, None]
+        xs, us, last, cot_all = forward(state, high, full, cot_strip)
     else:
         columns = lax.all_gather(weight, "dp", axis=0, tiled=True)
         full = lax.all_gather(columns, "mp", axis=1, tiled=True)
-    tables = lax.all_gather(destination, "dp", axis=1, tiled=True)
-    cot_strip = lax.dynamic_slice_in_dim(cotangent, core * strip, strip, 1)
-    cot_all = lax.all_gather(cot_strip, "dp", axis=0, tiled=True)
+        tables = lax.all_gather(destination, "dp", axis=1, tiled=True)
+        cot_all = lax.all_gather(cot_strip, "dp", axis=0, tiled=True)
     place = pick(tables[2], pick(tables[1], destination[0]))
     own = me * rows + jnp.arange(rows, dtype=jnp.int32)
     source = find(tables[0], find(tables[1], find(tables[2], own)))
     cot_rows = lax.all_gather(take_rows(place, cot_all), "mp", axis=1, tiled=True)
     cot = lax.dynamic_slice_in_dim(cot_rows, core * part, part, 0)
-    state = lax.dynamic_slice_in_dim(hidden_in, core * part, part, 0)
-    levels = lax.dynamic_slice_in_dim(depth, core * part, part, 0)
-    last, grad, left, right = recursions(state, levels, cot, full)
-    last_all = lax.all_gather(last, "dp", axis=0, tiled=True)
+    if square:
+        grad, left_all, right_half, last_all = backward(xs, us, high, cot, full, last)
+    else:
+        last, grad, left, right = recursions(state, levels, cot, full)
+        last_all = lax.all_gather(last, "dp", axis=0, tiled=True)
+        left_all = lax.all_gather(left, "mp", axis=0, tiled=True)
+        right_all = lax.all_gather(right, "mp", axis=0, tiled=True)
+        right_half = lax.dynamic_slice_in_dim(right_all, core * half_inner, half_inner, 1)
     owner, offset = source // rows, source % rows
     slot = jnp.where(offset // part == core, owner * part + offset % part, -1)
     final = lax.psum(take_rows(slot, last_all), "mp")
     grad_in = lax.all_gather(grad, "mp", axis=0, tiled=True)
-    left_all = lax.all_gather(left, "mp", axis=0, tiled=True)
-    right_all = lax.all_gather(right, "mp", axis=0, tiled=True)
-    right_half = lax.dynamic_slice_in_dim(right_all, core * half_inner, half_inner, 1)
     grad_weight = lax.dot_general(
         left_all, right_half, (((0,), (0,)), ((), ())), preferred_element_type=jnp.float32
     ).astype(jnp.bfloat16)

time: 269 us -> 229 us (0.85)
  Pallas kernels: 105 us -> 188 us
  matrix products: 55.5 us -> 12.3 us
  blocking collectives: 44.5 us -> 4.36 us
  waiting for transfers between devices: 36.3 us -> 0.04 us
  other arithmetic: 5.29 us -> 2.01 us
    pallas_call x1 -> x3, Pallas kernels: 56.8 us -> 141 us  [the longest x1 49.1 us: gather_weight(): pl.pallas_call(gather_kernel, out_shape=(jax.ShapeDtypeStruct((4, 2, 2, r...]
    dot_general x12 -> x0, matrix products: 42.6 us -> none  [the longest x3 13.5 us: recursions(): jnp.dot(grad_branch, weight, preferred_element_type=jnp.float32)]
    all_gather x1 -> x0, blocking collectives: 39.7 us -> none  [body(): tables = lax.all_gather(destination, 'dp', axis=1, tiled=True)]
    all_gather x4 -> x0, waiting for transfers between devices: 36.2 us -> none  [the longest x1 14.7 us: body(): right_all = lax.all_gather(right, 'mp', axis=0, tiled=True)]
    unnamed x27 -> x9, local copies, waits for them, and re-layouts: 6.66 us -> 5.1 us
  transfers between devices with their start and end apart: 5 -> 1, of which waited for: 3 -> 0; matrix products, arithmetic and copies ran while one was open for 23% -> 2% of each run, Pallas kernels for 39% -> 21%
where the time goes in v3:
time: 229 us; the launch traced here: 228 us
  Pallas kernels  188 us (82%)
  between operations  14.1 us (6%)
  matrix products  12.3 us (5%)
  local copies, waits for them, and re-layouts  6.97 us (3%)
  blocking collectives  4.36 us (2%)
    pallas_call x1, Pallas kernels, gather_weight(): pl.pallas_call(gather_kernel, out_shape=(jax.ShapeDtypeStruct((4, 2, 2, r...  49.1 us
    pallas_call x1, Pallas kernels, scatter_grad(): pl.pallas_call(scatter_kernel, out_shape=jax.ShapeDtypeStruct((rows, widt...  47.4 us
    pallas_call x1, Pallas kernels, backward(): pl.pallas_call(backward_kernel, out_shape=(jax.ShapeDtypeStruct((rows, wi...  46.2 us
    pallas_call x1, Pallas kernels, forward(): pl.pallas_call(forward_kernel, out_shape=(jax.ShapeDtypeStruct((3, rows,...  45.6 us
    dot_general x2, matrix products, take_rows(): jnp.dot((ids == index[:, None]).astype(jnp.bfloat16), table, preferred_el...  6.69 us
    dot_general x1, matrix products, body(): lax.dot_general(left_all, right_half, (((0,), (0,)), ((), ())), preferred...  5.63 us
    unnamed x9, local copies, waits for them, and re-layouts  5.1 us
  transfers between devices with their start and end apart: 1, of which 0 were waited for; matrix products, arithmetic and copies ran while one was open for 2% of the time, Pallas kernels for 21%

profile of v3, /device:TPU:0, one launch (start us, length us, event | category | flops | bytes accessed | tf_op | source)
XLA Modules:
  0.0 228.2 jit_solution(7106582231100209040)
XLA Ops:
  7.2 0.0 copy-start
  7.2 0.0 all-reduce.2.cloned.1.call-start
  7.2 0.7 slice_bitcast_fusion
  8.0 0.7 convert_bitcast_fusion
  8.7 0.1 copy.10.levels
  8.8 0.0 copy-done
  8.8 0.0 copy-start.1
  8.8 0.9 copy-done.1
  9.8 0.0 copy-start.2
  9.8 0.7 copy-done.2
  10.5 49.1 %shard_map.76 = (bf16[4,2,2,128,2048]{4,3,2,1,0:T(8,128)(2,1)}, s32[4,2,2,3,128]{4,3,2,1,0:T(4,128)S(1)}) custom-call(bf16[128,1024]{1,0:T(8,128)(2,1)S(1)} %copy-done.1, s32[3,128]{1,0:T(4,128)S(1)} %copy-done.2), custom_call_target="tpu_custom_call" | custom-call | bytes 100000000 | tf_op jit(solution)/shard_map/pallas_call | solution.py:239
  59.6 0.3 select_reduce_fusion.4
  59.9 0.4 select_reduce_fusion.3
  60.3 0.3 select_reduce_fusion
  60.6 0.3 select_reduce_fusion.2
  60.9 1.0 constant_dynamic-slice_fusion.block
  61.9 45.6 %shard_map.77 = (bf16[3,64,2048]{2,1,0:T(8,128)(2,1)S(1)}, f32[3,64,2048]{2,1,0:T(8,128)S(1)}, bf16[64,2048]{1,0:T(8,128)(2,1)S(1)}, bf16[4,2,2,128,1024]{4,3,2,1,0:T(8,128)(2,1)}) custom-call(bf16[64,2048]{1,0:T(8,128)(2,1)S(1)} %constant_dynamic-slice_fusion.1.state, f32[64,1]{1,0:T(8,128)S(1)} %copy.10.levels, bf16[2048,2048]{1,0:T(8,128)(2,1)} %bitcast.24, ...), custom_call_target="tpu_custom_call" | custom-call | tf_op jit(solution)/shard_map/pallas_call | solution.py:297
  107.5 2.9 %convolution_convert_fusion.1 = bf16[128,1024]{1,0:T(8,128)(2,1)S(1)} fusion(bf16[2048,1024]{1,0:T(8,128)(2,1)} %bitcast.27, s32[128]{0:T(128)S(1)} %select_reduce_fusion), kind=kOutput, calls=%fused_computation.2 | convolution fusion | flops 537264128 | bytes 4456960 | tf_op jit(solution)/shard_map/dot_general | solution.py:520
  110.4 2.2 all_gather.6
  112.6 46.2 %shard_map.78 = (bf16[64,2048]{1,0:T(8,128)(2,1)S(1)}, bf16[2,6,64,2048]{3,2,1,0:T(8,128)(2,1)}, bf16[2,6,64,1024]{3,2,1,0:T(8,128)(2,1)S(1)}, bf16[4,2,2,64,2048]{4,3,2,1,0:T(8,128)(2,1)}) custom-call(bf16[3,64,2048]{2,1,0:T(8,128)(2,1)S(1)} %get-tuple-element.15.xs, f32[3,64,2048]{2,1,0:T(8,128)S(1)} %get-tuple-element.16.us, f32[64,1]{1,0:T(8,128)S(1)} %copy.10.levels, ...), custom_call_target="tpu_custom_call" | custom-call | tf_op jit(solution)/shard_map/pallas_call | solution.py:369
  158.9 3.7 %convolution_convert_fusion = bf16[128,2048]{1,0:T(8,128)(2,1)} fusion(bf16[1024,2048]{1,0:T(8,128)(2,1)} %bitcast.26, s32[128]{0:T(128)S(1)} %compare_select_fusion), kind=kOutput, calls=%fused_computation.1 | convolution fusion | flops 537264128 | bytes 4719104 | tf_op jit(solution)/shard_map/dot_general | solution.py:520
  162.6 0.0 all-reduce.2.cloned.1.call-update
  162.6 5.6 %bitcast_convert_fusion = bf16[2048,1024]{1,0:T(8,128)(2,1)S(1)} fusion(bf16[2,6,64,2048]{3,2,1,0:T(8,128)(2,1)} %get-tuple-element.21, bf16[2,6,64,1024]{3,2,1,0:T(8,128)(2,1)S(1)} %get-tuple-element.22), kind=kOutput, calls=%fused_computation | convolution fusion | flops 3223322624 | bytes 8912896 | tf_op jit(solution)/shard_map/dot_general | solution.py:595
  168.3 2.2 all_gather.7
  170.5 47.4 %shard_map.79 = f32[128,1024]{1,0:T(8,128)S(1)} custom-call(bf16[4,2,2,128,1024]{4,3,2,1,0:T(8,128)(2,1)S(1)} %bitcast.22), custom_call_target="tpu_custom_call" | custom-call | bytes 100000000 | tf_op jit(solution)/shard_map/pallas_call | solution.py:485
  217.9 0.0 all-reduce.2.cloned.1.call-done
  217.9 1.9 copy.16
  219.8 0.8 copy.17
  220.6 0.8 copy.18
  (5 shorter events, 0.1 us)
Async XLA Ops:
  7.2 1.6 copy-start
  7.2 210.7 %all-reduce.2.cloned.1.call-start = ((), (), s32[]{:S(2)}) async-start(), calls=%async_computation | async-start | bytes 1048576 | tf_op jit(solution)/shard_map/psum | solution.py:593
  8.8 1.0 copy-start.1
  9.8 0.7 copy-start.2
Sparse Core Ops, SparseCore 0:
  162.8 17.8 all-reduce.1

commit v4 on v3

--- a/solution.py
+++ b/solution.py
@@ -58,7 +58,7 @@
         self.me, self.core = lax.axis_index("dp"), lax.axis_index("mp")
         self.z, self.y, self.x = place_of(self.me)
         self.width = block.shape[1]
-        self.half = self.width // len(paths)
+        self.half = self.width // max(1, len(paths))
         self.sibling = (self.me, 1 - self.core)
         me, x, y = self.me, self.x, self.y
         self.across = ((me + 1 - 2 * x, self.core), (me + 2 - 4 * y, self.core))
@@ -203,6 +203,78 @@
                 landed(self.whole(zp), self.sems[2].at[zp])
 
 
+class Line(Relay):
+    def __init__(self, block, out, sems):
+        super().__init__(block, out, sems, paths=())
+
+    def whole(self, zp, core=None):
+        rows = self.block.shape[0]
+        return self.out.at[pl.ds(zp * rows, rows)]
+
+    def spread(self, zp, own):
+        return
+
+    def each(self, k, act):
+        return
+
+
+class Plane:
+    def __init__(self, give, take, keep, pass_on, accept, sems):
+        self.give, self.take, self.keep = give, take, keep
+        self.pass_on, self.accept, self.sems = pass_on, accept, sems
+        me, core = lax.axis_index("dp"), lax.axis_index("mp")
+        _, self.y, self.x = place_of(me)
+        self.across = ((me + 1 - 2 * self.x, core), (me + 2 - 4 * self.y, core))
+        self.rows, self.half = keep.shape[2], keep.shape[3]
+
+    def picked(self, sel, zone, yp, xp, h):
+        slots = sel[pl.ds((yp * 2 + xp) * self.rows, self.rows), :]
+        ids = lax.broadcasted_iota(jnp.int32, (self.rows, zone.shape[0]), 1)
+        onehot = (ids == slots).astype(jnp.float32).astype(jnp.bfloat16)
+        cols = zone[:, pl.ds(h * self.half, self.half)]
+        return jnp.dot(onehot, cols, preferred_element_type=jnp.float32).astype(jnp.bfloat16)
+
+    def first(self, sel, zone):
+        y, x = self.y, self.x
+        for h in range(2):
+            for q in range(2):
+                yp, xp = (q, 1 - x) if h == 0 else (1 - y, q)
+                self.give[h, q] = self.picked(sel, zone, yp, xp, h)
+            push(self.give.at[h], self.take.at[h], self.sems[0].at[h], self.sems[1].at[h], self.across[h])
+        for h in range(2):
+            for q in range(2):
+                yp, xp = (q, x) if h == 0 else (y, q)
+                self.keep[h, q] = self.picked(sel, zone, yp, xp, h)
+
+    def joined(self, h, q):
+        return self.keep[h, q].astype(jnp.float32) + self.take[h, q].astype(jnp.float32)
+
+    def second(self):
+        for h in range(2):
+            landed(self.take.at[h], self.sems[1].at[h])
+            far = 1 - self.y if h == 0 else 1 - self.x
+            self.pass_on[h] = self.joined(h, far).astype(jnp.bfloat16)
+            push(
+                self.pass_on.at[h], self.accept.at[h], self.sems[2].at[h], self.sems[3].at[h],
+                self.across[1 - h],
+            )
+
+    def third(self, strip):
+        for h in range(2):
+            landed(self.accept.at[h], self.sems[3].at[h])
+            near = self.y if h == 0 else self.x
+            value = self.joined(h, near) + self.accept[h].astype(jnp.float32)
+            strip[:, pl.ds(h * self.half, self.half)] = value.astype(jnp.bfloat16)
+            landed(self.give.at[h], self.sems[0].at[h])
+            landed(self.pass_on.at[h], self.sems[2].at[h])
+
+
+def plane_scratch(rows, half):
+    two = pltpu.VMEM((2, 2, rows, half), jnp.bfloat16)
+    one = pltpu.VMEM((2, rows, half), jnp.bfloat16)
+    return [two, two, two, one, one] + [pltpu.SemaphoreType.DMA((2,))] * 4
+
+
 def relay_sems(beside):
     dma = pltpu.SemaphoreType.DMA
     base = [dma(()), dma((4,)), dma((4,)), dma((4,))] + [dma((2, 4))] * 4
@@ -214,17 +286,21 @@
     greet(*place_of(me), core)
 
 
-def gather_kernel(block, table, out, tables, *sems):
+def gather_kernel(block, table, strip, out, tables, zone, *sems):
     main = Relay(block, out, sems[:14], beside=True)
-    small = Relay(table, tables, sems[14:], paths=(0,))
+    small = Relay(table, tables, sems[14:22], paths=(0,))
+    line = Line(strip, zone, sems[22:26])
     enter()
     main.start()
     small.start()
+    line.start()
     for k in range(1, 4):
         main.step(k)
         small.step(k)
+        line.step(k)
     small.finish()
     main.finish()
+    line.finish()
 
 
 def params(number):
@@ -233,23 +309,24 @@
     )
 
 
-def gather_weight(block, table):
+def gather_weight(block, table, strip):
     rows, width = block.shape
     anywhere = pl.BlockSpec(memory_space=pl.ANY)
-    out, tables = pl.pallas_call(
+    out, tables, zone = pl.pallas_call(
         gather_kernel,
         out_shape=(
             jax.ShapeDtypeStruct((4, 2, 2, rows, 2 * width), block.dtype),
             jax.ShapeDtypeStruct((4, 2, 2) + table.shape, table.dtype),
+            jax.ShapeDtypeStruct((4 * strip.shape[0], strip.shape[1]), strip.dtype),
         ),
-        in_specs=[anywhere, anywhere],
-        out_specs=(anywhere, anywhere),
-        scratch_shapes=relay_sems(True) + relay_sems(False),
+        in_specs=[anywhere] * 3,
+        out_specs=(anywhere,) * 3,
+        scratch_shapes=relay_sems(True) + relay_sems(False) + relay_sems(False)[:4],
         compiler_params=params(0),
         cost_estimate=pl.CostEstimate(flops=0, bytes_accessed=100_000_000, transcendentals=0),
-    )(block, table)
+    )(block, table, strip)
     tables = tables.reshape((16,) + table.shape).transpose(1, 0, 2).reshape(table.shape[0], -1)
-    return out.reshape(16 * rows, 2 * width), tables
+    return out.reshape(16 * rows, 2 * width), tables, zone
 
 
 def times(left, weight, out):
@@ -272,10 +349,23 @@
     return lax.rsqrt(jnp.mean(state_f * state_f, axis=-1, keepdims=True) + 1e-06)
 
 
-def forward_kernel(state, levels, weight, block, xs, us, last, out, low, wide, *sems):
-    relay = Relay(block, out, sems)
+def recur_kernel(
+    state, levels, weight, cot_zone, cot_sel, last_sel, final, grad, lefts, rights,
+    xs, us, low, wide, dx, full, last, cot, cot_strip, last_strip, last_zone, end_strip, *sems
+):
+    cots, ends = Plane(*sems[:5], sems[5:9]), Plane(*sems[9:14], sems[14:18])
+    line = Line(last_strip, last_zone, sems[18:22])
+    lsend, lrecv, rsend, rrecv, esend, erecv = sems[22:]
+    core, sibling = line.core, line.sibling
+    part, strip, half = last.shape[0], last_strip.shape[1], rights.shape[3]
+    mine = pl.ds(pl.multiple_of(core * strip, strip), strip)
+    theirs = pl.ds(pl.multiple_of((1 - core) * strip, strip), strip)
+    own_inner = pl.ds(pl.multiple_of(core * half, half), half)
+    other_inner = pl.ds(pl.multiple_of((1 - core) * half, half), half)
+    own_rows = pl.ds(pl.multiple_of(core * part, part), part)
+    other_rows = pl.ds(pl.multiple_of((1 - core) * part, part), part)
     enter()
-    relay.start()
+    cots.first(cot_sel, cot_zone)
     last[...] = state[...]
     for step in range(3):
         xs[step] = last[...]
@@ -287,52 +377,23 @@
         times_transposed(low, weight, wide)
         active = (levels[...] >= step + 1).astype(jnp.float32)
         last[...] = (last[...].astype(jnp.float32) + active * wide[...]).astype(jnp.bfloat16)
-        relay.step(step + 1)
-    relay.finish()
-
-
-def forward(state, levels, weight, block):
-    rows, width = state.shape
-    vmem, anywhere = pl.BlockSpec(memory_space=pltpu.VMEM), pl.BlockSpec(memory_space=pl.ANY)
-    xs, us, last, out = pl.pallas_call(
-        forward_kernel,
-        out_shape=(
-            jax.ShapeDtypeStruct((3, rows, width), jnp.bfloat16),
-            jax.ShapeDtypeStruct((3, rows, width), jnp.float32),
-            jax.ShapeDtypeStruct((rows, width), jnp.bfloat16),
-            jax.ShapeDtypeStruct((4, 2, 2) + block.shape, block.dtype),
-        ),
-        in_specs=[vmem, vmem, vmem, anywhere],
-        out_specs=(vmem, vmem, vmem, anywhere),
-        scratch_shapes=[
-            pltpu.VMEM((rows, width), jnp.bfloat16),
-            pltpu.VMEM((rows, width), jnp.float32),
-        ]
-        + relay_sems(False),
-        compiler_params=params(2),
-    )(state, levels, weight, block)
-    return xs, us, last, out.reshape(16 * block.shape[0], block.shape[1])
-
-
-def backward_kernel(
-    xs, us, levels, cot, weight, block, grad, lefts, rights, out,
-    full, wide, dx, lsend, lrecv, rsend, rrecv, *sems
-):
-    relay = Relay(block, out, sems)
-    core, sibling = relay.core, relay.sibling
-    half = rights.shape[3]
-    mine = pl.ds(pl.multiple_of(core * half, half), half)
-    theirs = pl.ds(pl.multiple_of((1 - core) * half, half), half)
-    enter()
-    relay.start()
+        if step == 0:
+            cots.second()
+        if step == 1:
+            cots.third(cot_strip)
+            push(cot_strip.at[other_rows], cot.at[:, mine], esend.at[0], erecv.at[0], sibling)
+            cot[:, mine] = cot_strip[own_rows, :]
+    push(last.at[:, theirs], last_strip.at[own_rows], esend.at[1], erecv.at[1], sibling)
+    last_strip[own_rows, :] = last[:, mine]
+    landed(cot.at[:, theirs], erecv.at[0])
     dx[...] = cot[...].astype(jnp.float32)
 
     def share(i):
         push(lefts.at[core, i], lefts.at[core, i], lsend.at[i], lrecv.at[i], sibling)
-        rights[core, i] = full[i, :, mine]
-        push(full.at[i, :, theirs], rights.at[core, i], rsend.at[i], rrecv.at[i], sibling)
-
-    for turn, step in enumerate((2, 1, 0)):
+        rights[core, i] = full[i, :, own_inner]
+        push(full.at[i, :, other_inner], rights.at[core, i], rsend.at[i], rrecv.at[i], sibling)
+
+    for step in (2, 1, 0):
         a, b = 2 * step, 2 * step + 1
         state_f = xs[step].astype(jnp.float32)
         rinv = scale_of(state_f)
@@ -340,6 +401,13 @@
         active = (levels[...] >= step + 1).astype(jnp.float32)
         lefts[core, b] = (active * dx[...]).astype(jnp.bfloat16)
         times(lefts.at[core, b], weight, wide)
+        if step == 2:
+            landed(last_strip.at[other_rows], erecv.at[1])
+            line.start()
+        if step == 1:
+            line.step(2)
+        if step == 0:
+            ends.second()
         inner = us[step]
         sigma = 1.0 / (1.0 + jnp.exp(-inner))
         full[b] = (inner * sigma).astype(jnp.bfloat16)
@@ -351,42 +419,67 @@
         mean = jnp.mean(wide[...] * state_f, axis=-1, keepdims=True)
         entry = dx[...] + rinv * wide[...] - state_f * (rinv * rinv * rinv * mean)
         dx[...] = entry.astype(jnp.bfloat16).astype(jnp.float32)
-        relay.step(turn + 1)
-    grad[...] = dx[...].astype(jnp.bfloat16)
+        if step == 2:
+            line.step(1)
+        if step == 1:
+            line.step(3)
+            line.finish()
+            ends.first(last_sel, last_zone)
+    grad[own_rows, :] = dx[...].astype(jnp.bfloat16)
+    push(grad.at[own_rows], grad.at[own_rows], esend.at[2], erecv.at[2], sibling)
+    ends.third(end_strip)
+    push(end_strip, final.at[:, mine], esend.at[3], erecv.at[3], sibling)
+    final[:, mine] = end_strip[...]
     for i in range(6):
         landed(lefts.at[1 - core, i], lrecv.at[i])
         landed(rights.at[1 - core, i], rrecv.at[i])
         landed(lefts.at[core, i], lsend.at[i])
-        landed(full.at[i, :, theirs], rsend.at[i])
-    relay.finish()
-
-
-def backward(xs, us, levels, cot, weight, block):
-    rows, width = cot.shape
-    half = weight.shape[1] // 2
-    vmem, anywhere = pl.BlockSpec(memory_space=pltpu.VMEM), pl.BlockSpec(memory_space=pl.ANY)
+        landed(full.at[i, :, other_inner], rsend.at[i])
+    landed(cot_strip.at[other_rows], esend.at[0])
+    landed(last.at[:, theirs], esend.at[1])
+    landed(grad.at[own_rows], esend.at[2])
+    landed(end_strip, esend.at[3])
+    landed(grad.at[other_rows], erecv.at[2])
+    landed(final.at[:, theirs], erecv.at[3])
+
+
+def recur(state, levels, weight, cot_zone, cot_sel, last_sel):
+    part, width = state.shape
+    rows, half, strip = 2 * part, weight.shape[1] // 2, width // 2
+    vmem = pl.BlockSpec(memory_space=pltpu.VMEM)
     dma = pltpu.SemaphoreType.DMA
-    grad, lefts, rights, out = pl.pallas_call(
-        backward_kernel,
+    low, high = jnp.bfloat16, jnp.float32
+    final, grad, lefts, rights = pl.pallas_call(
+        recur_kernel,
         out_shape=(
-            jax.ShapeDtypeStruct((rows, width), jnp.bfloat16),
-            jax.ShapeDtypeStruct((2, 6, rows, width), jnp.bfloat16),
-            jax.ShapeDtypeStruct((2, 6, rows, half), jnp.bfloat16),
-            jax.ShapeDtypeStruct((4, 2, 2) + block.shape, block.dtype),
+            jax.ShapeDtypeStruct((rows, width), low),
+            jax.ShapeDtypeStruct((rows, width), low),
+            jax.ShapeDtypeStruct((2, 6, part, width), low),
+            jax.ShapeDtypeStruct((2, 6, part, half), low),
         ),
-        in_specs=[vmem] * 5 + [anywhere],
-        out_specs=(vmem, vmem, vmem, anywhere),
+        in_specs=[vmem] * 6,
+        out_specs=(vmem,) * 4,
         scratch_shapes=[
-            pltpu.VMEM((6, rows, 2 * half), jnp.bfloat16),
-            pltpu.VMEM((rows, width), jnp.float32),
-            pltpu.VMEM((rows, width), jnp.float32),
+            pltpu.VMEM((3, part, width), low),
+            pltpu.VMEM((3, part, 2 * half), high),
+            pltpu.VMEM((part, 2 * half), low),
+            pltpu.VMEM((part, width), high),
+            pltpu.VMEM((part, width), high),
+            pltpu.VMEM((6, part, 2 * half), low),
+            pltpu.VMEM((part, width), low),
+            pltpu.VMEM((part, width), low),
+            pltpu.VMEM((rows, strip), low),
+            pltpu.VMEM((rows, strip), low),
+            pltpu.VMEM((4 * rows, strip), low),
+            pltpu.VMEM((rows, strip), low),
         ]
+        + plane_scratch(rows, strip // 2) * 2
+        + relay_sems(False)[:4]
         + [dma((6,))] * 4
-        + relay_sems(False),
-        compiler_params=params(3),
-    )(xs, us, levels, cot, weight, block)
-    merged = out.reshape(16 * block.shape[0], block.shape[1])
-    return grad, lefts.reshape(-1, width), rights.reshape(-1, half), merged
+        + [dma((4,))] * 2,
+        compiler_params=params(2),
+    )(state, levels, weight, cot_zone, cot_sel, last_sel)
+    return final, grad, lefts.reshape(-1, width), rights.reshape(-1, half)
 
 
 def scatter_kernel(
@@ -556,48 +649,62 @@
     return final, grad.astype(jnp.bfloat16), jnp.concatenate(lefts), jnp.concatenate(rights)
 
 
+def from_column(position, rows, me):
+    owner = position // rows
+    return jnp.where(owner % 4 == me % 4, owner // 4 * rows + position % rows, -1)[:, None]
+
+
 def body(hidden_in, depth, destination, weight, cotangent):
     rows, width = hidden_in.shape
     half_inner = weight.shape[1]
     cores = lax.axis_size("mp")
     me, core = lax.axis_index("dp"), lax.axis_index("mp")
     part, strip = rows // cores, width // cores
-    square = lax.axis_size("dp") == 16 and cores == 2
     state = lax.dynamic_slice_in_dim(hidden_in, core * part, part, 0)
     levels = lax.dynamic_slice_in_dim(depth, core * part, part, 0)
     cot_strip = lax.dynamic_slice_in_dim(cotangent, core * strip, strip, 1)
-    if square:
-        full, tables = gather_weight(weight, destination)
-        high = levels.astype(jnp.float32)[:, None]
-        xs, us, last, cot_all = forward(state, high, full, cot_strip)
-    else:
-        columns = lax.all_gather(weight, "dp", axis=0, tiled=True)
-        full = lax.all_gather(columns, "mp", axis=1, tiled=True)
-        tables = lax.all_gather(destination, "dp", axis=1, tiled=True)
-        cot_all = lax.all_gather(cot_strip, "dp", axis=0, tiled=True)
+    contract = (((0,), (0,)), ((), ()))
+    if lax.axis_size("dp") == 16 and cores == 2:
+        full, tables, cot_zone = gather_weight(weight, destination, cot_strip)
+        start = me // 4 * 4 * rows
+        leaving = lax.dynamic_slice_in_dim(tables[0], start, 4 * rows, 0)
+        place = pick(tables[2], pick(tables[1], leaving))
+        own = start + jnp.arange(4 * rows, dtype=jnp.int32)
+        source = find(tables[0], find(tables[1], find(tables[2], own)))
+        final, grad_in, left_all, right_half = recur(
+            state,
+            levels.astype(jnp.float32)[:, None],
+            full,
+            cot_zone,
+            from_column(place, rows, me),
+            from_column(source, rows, me),
+        )
+        partial = lax.dot_general(
+            left_all, right_half, contract, preferred_element_type=jnp.float32
+        ).astype(jnp.bfloat16)
+        return final, grad_in, scatter_grad(partial)
+    columns = lax.all_gather(weight, "dp", axis=0, tiled=True)
+    full = lax.all_gather(columns, "mp", axis=1, tiled=True)
+    tables = lax.all_gather(destination, "dp", axis=1, tiled=True)
+    cot_all = lax.all_gather(cot_strip, "dp", axis=0, tiled=True)
     place = pick(tables[2], pick(tables[1], destination[0]))
     own = me * rows + jnp.arange(rows, dtype=jnp.int32)
     source = find(tables[0], find(tables[1], find(tables[2], own)))
     cot_rows = lax.all_gather(take_rows(place, cot_all), "mp", axis=1, tiled=True)
     cot = lax.dynamic_slice_in_dim(cot_rows, core * part, part, 0)
-    if square:
-        grad, left_all, right_half, last_all = backward(xs, us, high, cot, full, last)
-    else:
-        last, grad, left, right = recursions(state, levels, cot, full)
-        last_all = lax.all_gather(last, "dp", axis=0, tiled=True)
-        left_all = lax.all_gather(left, "mp", axis=0, tiled=True)
-        right_all = lax.all_gather(right, "mp", axis=0, tiled=True)
-        right_half = lax.dynamic_slice_in_dim(right_all, core * half_inner, half_inner, 1)
+    last, grad, left, right = recursions(state, levels, cot, full)
+    last_all = lax.all_gather(last, "dp", axis=0, tiled=True)
+    left_all = lax.all_gather(left, "mp", axis=0, tiled=True)
+    right_all = lax.all_gather(right, "mp", axis=0, tiled=True)
+    right_half = lax.dynamic_slice_in_dim(right_all, core * half_inner, half_inner, 1)
     owner, offset = source // rows, source % rows
     slot = jnp.where(offset // part == core, owner * part + offset % part, -1)
     final = lax.psum(take_rows(slot, last_all), "mp")
     grad_in = lax.all_gather(grad, "mp", axis=0, tiled=True)
-    grad_weight = lax.dot_general(
-        left_all, right_half, (((0,), (0,)), ((), ())), preferred_element_type=jnp.float32
+    partial = lax.dot_general(
+        left_all, right_half, contract, preferred_element_type=jnp.float32
     ).astype(jnp.bfloat16)
-    if square:
-        return final, grad_in, scatter_grad(grad_weight)
-    owned = lax.psum_scatter(grad_weight, "dp", scatter_dimension=0, tiled=True)
+    owned = lax.psum_scatter(partial, "dp", scatter_dimension=0, tiled=True)
     return final, grad_in, owned.astype(jnp.float32)
 
 

time: 229 us -> 180 us (0.79)
  Pallas kernels: 188 us -> 162 us
  between operations: 14.1 us -> 0.76 us
  matrix products: 12.3 us -> 5.6 us
  blocking collectives: 4.36 us -> 0 us
  other arithmetic: 2.01 us -> 5.17 us
    pallas_call x2 -> x1, Pallas kernels: 91.8 us -> 61.1 us  [recur(): pl.pallas_call(recur_kernel, out_shape=(jax.ShapeDtypeStruct((rows, width...]
    dot_general x3 -> x1, matrix products: 12.3 us -> 5.6 us  [body(): lax.dot_general(left_all, right_half, contract, preferred_element_type=jn...]
    pallas_call x1, Pallas kernels: 49.1 us -> 54.8 us  [gather_weight(): pl.pallas_call(gather_kernel, out_shape=(jax.ShapeDtypeStruct((4, 2, 2, r...]
    all_gather x2 -> x0, blocking collectives: 4.36 us -> none  [the longest x1 2.18 us: body(): lax.all_gather(take_rows(place, cot_all), 'mp', axis=1, tiled=True)]
    reduce_sum x3, other arithmetic: 0.97 us -> 3.42 us  [find(): return jnp.sum(jnp.where(table[None, :] == value[:, None], ids, 0), axis=1)]
  transfers between devices with their start and end apart: 1 -> 0, of which waited for: 0 -> 0; matrix products, arithmetic and copies ran while one was open for 2% -> 0% of each run, Pallas kernels for 21% -> 0%
where the time goes in v4:
time: 180 us; the launch traced here: 179 us
  Pallas kernels  162 us (90%)
  local copies, waits for them, and re-layouts  5.63 us (3%)
  matrix products  5.6 us (3%)
  other arithmetic  5.17 us (3%)
    pallas_call x1, Pallas kernels, recur(): pl.pallas_call(recur_kernel, out_shape=(jax.ShapeDtypeStruct((rows, width...  61.1 us
    pallas_call x1, Pallas kernels, gather_weight(): pl.pallas_call(gather_kernel, out_shape=(jax.ShapeDtypeStruct((4, 2, 2, r...  54.8 us
    pallas_call x1, Pallas kernels, scatter_grad(): pl.pallas_call(scatter_kernel, out_shape=jax.ShapeDtypeStruct((rows, widt...  46.3 us
    dot_general x1, matrix products, body(): lax.dot_general(left_all, right_half, contract, preferred_element_type=jn...  5.6 us
    unnamed x9, local copies, waits for them, and re-layouts  4.15 us

profile of v4, /device:TPU:0, one launch (start us, length us, event | category | flops | bytes accessed | tf_op | source)
XLA Modules:
  0.0 179.3 jit_solution(12335836905364952313)
XLA Ops:
  0.6 0.0 copy-start
  0.7 0.8 convert_bitcast_fusion
  1.5 0.1 copy.26.levels
  1.6 0.1 copy-done
  1.7 1.0 constant_dynamic-slice_fusion.strip
  2.7 0.0 copy-start.1
  2.7 0.9 copy-done.1
  3.6 0.0 copy-start.2
  3.6 0.7 copy-done.2
  4.3 54.8 %shard_map.76 = (bf16[4,2,2,128,2048]{4,3,2,1,0:T(8,128)(2,1)}, s32[4,2,2,3,128]{4,3,2,1,0:T(4,128)S(1)}, bf16[512,1024]{1,0:T(8,128)(2,1)S(1)}) custom-call(bf16[128,1024]{1,0:T(8,128)(2,1)S(1)} %copy-done.1, s32[3,128]{1,0:T(4,128)S(1)} %copy-done.2, bf16[128,1024]{1,0:T(8,128)(2,1)S(1)} %constant_dynamic-slice_fusion.strip), custom_call_target="tpu_custom_call" | custom-call | bytes 100000000 | tf_op jit(solution)/shard_map/pallas_call | solution.py:315
  59.1 0.7 select_reduce_fusion.2
  59.9 0.1 dynamic_slice.15
  59.9 1.4 select_reduce_fusion.1
  61.3 1.3 select_reduce_fusion
  62.6 0.2 copy.18
  62.8 0.5 fusion.3.cot_sel
  63.3 0.1 copy.22
  63.4 0.5 fusion.7.last_sel
  63.9 61.1 %shard_map.77 = (bf16[128,2048]{1,0:T(8,128)(2,1)S(1)}, bf16[128,2048]{1,0:T(8,128)(2,1)S(1)}, bf16[2,6,64,2048]{3,2,1,0:T(8,128)(2,1)}, bf16[2,6,64,1024]{3,2,1,0:T(8,128)(2,1)S(1)}) custom-call(bf16[64,2048]{1,0:T(8,128)(2,1)S(1)} %constant_dynamic-slice_fusion.1.state, f32[64,1]{1,0:T(8,128)S(1)} %copy.26.levels, bf16[2048,2048]{1,0:T(8,128)(2,1)} %bitcast.20, ...), custom_call_target="tpu_custom_call" | custom-call | tf_op jit(solution)/shard_map/pallas_call | solution.py:452
  125.0 5.6 %bitcast_convert_fusion = bf16[2048,1024]{1,0:T(8,128)(2,1)S(1)} fusion(bf16[2,6,64,2048]{3,2,1,0:T(8,128)(2,1)} %get-tuple-element.15, bf16[2,6,64,1024]{3,2,1,0:T(8,128)(2,1)S(1)} %get-tuple-element.16), kind=kOutput, calls=%fused_computation | convolution fusion | flops 3223322624 | bytes 8912896 | tf_op jit(solution)/shard_map/dot_general | solution.py:682
  130.6 46.3 %shard_map.78 = f32[128,1024]{1,0:T(8,128)S(1)} custom-call(bf16[4,2,2,128,1024]{4,3,2,1,0:T(8,128)(2,1)S(1)} %bitcast.18), custom_call_target="tpu_custom_call" | custom-call | bytes 100000000 | tf_op jit(solution)/shard_map/pallas_call | solution.py:578
  176.9 0.8 copy.31
  177.7 0.8 copy.32
  178.5 0.8 copy.33
  (3 shorter events, 0.0 us)
Async XLA Ops:
  0.6 1.1 copy-start
  2.7 1.0 copy-start.1
  3.6 0.7 copy-start.2

commit v5 on v4

--- a/solution.py
+++ b/solution.py
@@ -176,9 +176,6 @@
         self.each(k - 1, self.second)
 
     def finish(self):
-        self.each(3, self.second)
-        for k in range(4):
-            self.each(k, self.third)
         z, other = self.z, 1 - self.core
         for zp in range(4):
             for h in self.paths:
@@ -293,12 +290,20 @@
     enter()
     main.start()
     small.start()
-    line.start()
     for k in range(1, 4):
         main.step(k)
         small.step(k)
-        line.step(k)
+    line.start()
+    main.each(3, main.second)
+    line.step(1)
+    small.each(3, small.second)
+    for k in range(4):
+        small.each(k, small.third)
     small.finish()
+    for k in range(4):
+        main.each(k, main.third)
+        if k in (0, 2):
+            line.step(2 + k // 2)
     main.finish()
     line.finish()
 
@@ -483,12 +488,13 @@
 
 
 def scatter_kernel(
-    d, out, btake, agive, atake, total, ugive, utake, dgive, dtake,
+    left, right, out, d, btake, agive, atake, total, ugive, utake, dgive, dtake,
     bsend, brecv, asend, arecv, usend, urecv, dsend, drecv,
 ):
     me, core = lax.axis_index("dp"), lax.axis_index("mp")
     z, y, x = place_of(me)
     half = d.shape[4] // 2
+    group = left.shape[1] // 4
     across = ((me + 1 - 2 * x, core), (me + 2 - 4 * y, core))
     greet(z, y, x, core)
     first = 3 * (1 - z // 2)
@@ -499,6 +505,11 @@
         return pl.ds(h * half, half)
 
     for zp in order:
+        span = pl.ds(pl.multiple_of(zp * group, group), group)
+        product = lax.dot_general(
+            left[:, span], right[...], (((0,), (0,)), ((), ())), preferred_element_type=jnp.float32
+        )
+        d[zp] = product.astype(d.dtype).reshape(d.shape[1:])
         push(d.at[zp, 1 - y, :, :, cols(0)], btake.at[0, zp], bsend.at[0, zp], brecv.at[0, zp], across[1])
         push(d.at[zp, :, 1 - x, :, cols(1)], btake.at[1, zp], bsend.at[1, zp], brecv.at[1, zp], across[0])
 
@@ -570,18 +581,19 @@
                 landed(dgive.at[h, zp], dsend.at[h, zp])
 
 
-def scatter_grad(partial):
-    rows, width = partial.shape[0] // 16, partial.shape[1]
+def scatter_grad(left, right):
+    rows, width = left.shape[1] // 16, right.shape[1]
     half = width // 2
     dma = pltpu.SemaphoreType.DMA
-    one = pltpu.VMEM((2, 4, rows, half), partial.dtype)
+    one = pltpu.VMEM((2, 4, rows, half), left.dtype)
     return pl.pallas_call(
         scatter_kernel,
         out_shape=jax.ShapeDtypeStruct((rows, width), jnp.float32),
-        in_specs=[pl.BlockSpec(memory_space=pltpu.VMEM)],
+        in_specs=[pl.BlockSpec(memory_space=pltpu.VMEM)] * 2,
         out_specs=pl.BlockSpec(memory_space=pltpu.VMEM),
         scratch_shapes=[
-            pltpu.VMEM((2, 4, 2, rows, half), partial.dtype),
+            pltpu.VMEM((4, 2, 2, rows, width), left.dtype),
+            pltpu.VMEM((2, 4, 2, rows, half), left.dtype),
             one,
             one,
             pltpu.VMEM((2, 4, rows, half), jnp.float32),
@@ -595,7 +607,7 @@
             collective_id=1, has_side_effects=True, vmem_limit_bytes=32 * 1024 * 1024
         ),
         cost_estimate=pl.CostEstimate(flops=0, bytes_accessed=100_000_000, transcendentals=0),
-    )(partial.reshape(4, 2, 2, rows, width))
+    )(left, right)
 
 
 def pick(table, index):
@@ -679,10 +691,7 @@
             from_column(place, rows, me),
             from_column(source, rows, me),
         )
-        partial = lax.dot_general(
-            left_all, right_half, contract, preferred_element_type=jnp.float32
-        ).astype(jnp.bfloat16)
-        return final, grad_in, scatter_grad(partial)
+        return final, grad_in, scatter_grad(left_all, right_half)
     columns = lax.all_gather(weight, "dp", axis=0, tiled=True)
     full = lax.all_gather(columns, "mp", axis=1, tiled=True)
     tables = lax.all_gather(destination, "dp", axis=1, tiled=True)

time: 180 us -> 183 us (1.017)
  Pallas kernels: 162 us -> 170 us
  matrix products: 5.6 us -> 0 us
  local copies, waits for them, and re-layouts: 5.63 us -> 7.51 us
    pallas_call x1, Pallas kernels: 54.8 us -> 61.1 us  [gather_weight(): pl.pallas_call(gather_kernel, out_shape=(jax.ShapeDtypeStruct((4, 2, 2, r...]
    dot_general x1 -> x0, matrix products: 5.6 us -> none  [body(): lax.dot_general(left_all, right_half, contract, preferred_element_type=jn...]
    pallas_call x1, Pallas kernels: 46.3 us -> 48.2 us  [scatter_grad(): pl.pallas_call(scatter_kernel, out_shape=jax.ShapeDtypeStruct((rows, widt...]
    unnamed x9 -> x11, local copies, waits for them, and re-layouts: 4.15 us -> 6.03 us
where the time goes in v5:
time: 183 us
  Pallas kernels  170 us (93%)
  local copies, waits for them, and re-layouts  7.51 us (4%)
  other arithmetic  5.17 us (3%)
    pallas_call x1, Pallas kernels, gather_weight(): pl.pallas_call(gather_kernel, out_shape=(jax.ShapeDtypeStruct((4, 2, 2, r...  61.1 us
    pallas_call x1, Pallas kernels, recur(): pl.pallas_call(recur_kernel, out_shape=(jax.ShapeDtypeStruct((rows, width...  60.3 us
    pallas_call x1, Pallas kernels, scatter_grad(): pl.pallas_call(scatter_kernel, out_shape=jax.ShapeDtypeStruct((rows, widt...  48.2 us
    unnamed x11, local copies, waits for them, and re-layouts  6.03 us

profile of v5, /device:TPU:0, one launch (start us, length us, event | category | flops | bytes accessed | tf_op | source)
XLA Modules:
  0.0 183.0 jit_solution(12287480620124195897)
XLA Ops:
  0.6 0.0 copy-start
  0.7 0.8 convert_bitcast_fusion
  1.5 0.1 copy.26.levels
  1.6 0.1 copy-done
  1.7 1.0 constant_dynamic-slice_fusion.strip
  2.7 0.0 copy-start.2
  2.7 0.9 copy-done.2
  3.6 0.0 copy-start.3
  3.6 0.7 copy-done.3
  4.3 61.1 %shard_map.76 = (bf16[4,2,2,128,2048]{4,3,2,1,0:T(8,128)(2,1)}, s32[4,2,2,3,128]{4,3,2,1,0:T(4,128)S(1)}, bf16[512,1024]{1,0:T(8,128)(2,1)S(1)}) custom-call(bf16[128,1024]{1,0:T(8,128)(2,1)S(1)} %copy-done.2, s32[3,128]{1,0:T(4,128)S(1)} %copy-done.3, bf16[128,1024]{1,0:T(8,128)(2,1)S(1)} %constant_dynamic-slice_fusion.strip), custom_call_target="tpu_custom_call" | custom-call | bytes 100000000 | tf_op jit(solution)/shard_map/pallas_call | solution.py:320
  65.5 0.7 select_reduce_fusion.2
  66.2 0.1 dynamic_slice.15
  66.3 1.4 select_reduce_fusion.1
  67.6 1.3 select_reduce_fusion
  69.0 0.2 copy.18
  69.1 0.5 fusion.3.cot_sel
  69.6 0.1 copy.22
  69.8 0.5 fusion.7.last_sel
  70.3 60.3 %shard_map.77 = (bf16[128,2048]{1,0:T(8,128)(2,1)S(1)}, bf16[128,2048]{1,0:T(8,128)(2,1)S(1)}, bf16[2,6,64,2048]{3,2,1,0:T(8,128)(2,1)}, bf16[2,6,64,1024]{3,2,1,0:T(8,128)(2,1)S(1)}) custom-call(bf16[64,2048]{1,0:T(8,128)(2,1)S(1)} %constant_dynamic-slice_fusion.1.state, f32[64,1]{1,0:T(8,128)S(1)} %copy.26.levels, bf16[2048,2048]{1,0:T(8,128)(2,1)} %bitcast.16, ...), custom_call_target="tpu_custom_call" | custom-call | tf_op jit(solution)/shard_map/pallas_call | solution.py:457
  130.6 0.0 copy-start.1
  130.6 1.9 %copy-done.1 = bf16[2,6,64,2048]{3,2,1,0:T(8,128)(2,1)S(1)} copy-done((bf16[2,6,64,2048]{3,2,1,0:T(8,128)(2,1)S(1)}, bf16[2,6,64,2048]{3,2,1,0:T(8,128)(2,1)}, u32[]{:S(2)}) %copy-start.1) | copy-done | bytes 3145752
  132.4 48.2 %shard_map.78 = f32[128,1024]{1,0:T(8,128)S(1)} custom-call(bf16[768,2048]{1,0:T(8,128)(2,1)S(1)} %bitcast.13, bf16[768,1024]{1,0:T(8,128)(2,1)S(1)} %bitcast.14), custom_call_target="tpu_custom_call" | custom-call | bytes 100000000 | tf_op jit(solution)/shard_map/pallas_call | solution.py:589
  180.7 0.8 copy.30
  181.5 0.8 copy.31
  182.2 0.8 copy.32
  (3 shorter events, 0.0 us)
Async XLA Ops:
  0.6 1.1 copy-start
  2.7 1.0 copy-start.2
  3.6 0.7 copy-start.3
  130.6 1.9 %copy-start.1 = (bf16[2,6,64,2048]{3,2,1,0:T(8,128)(2,1)S(1)}, bf16[2,6,64,2048]{3,2,1,0:T(8,128)(2,1)}, u32[]{:S(2)}) copy-start(bf16[2,6,64,2048]{3,2,1,0:T(8,128)(2,1)} %get-tuple-element.15) | copy-start | bytes 9437188

commit v6 on v5

--- a/solution.py
+++ b/solution.py
@@ -283,29 +283,23 @@
     greet(*place_of(me), core)
 
 
-def gather_kernel(block, table, strip, out, tables, zone, *sems):
+def gather_kernel(block, table, out, tables, *sems):
     main = Relay(block, out, sems[:14], beside=True)
     small = Relay(table, tables, sems[14:22], paths=(0,))
-    line = Line(strip, zone, sems[22:26])
     enter()
     main.start()
     small.start()
     for k in range(1, 4):
         main.step(k)
         small.step(k)
-    line.start()
     main.each(3, main.second)
-    line.step(1)
     small.each(3, small.second)
     for k in range(4):
         small.each(k, small.third)
     small.finish()
     for k in range(4):
         main.each(k, main.third)
-        if k in (0, 2):
-            line.step(2 + k // 2)
     main.finish()
-    line.finish()
 
 
 def params(number):
@@ -314,24 +308,23 @@
     )
 
 
-def gather_weight(block, table, strip):
+def gather_weight(block, table):
     rows, width = block.shape
     anywhere = pl.BlockSpec(memory_space=pl.ANY)
-    out, tables, zone = pl.pallas_call(
+    out, tables = pl.pallas_call(
         gather_kernel,
         out_shape=(
             jax.ShapeDtypeStruct((4, 2, 2, rows, 2 * width), block.dtype),
             jax.ShapeDtypeStruct((4, 2, 2) + table.shape, table.dtype),
-            jax.ShapeDtypeStruct((4 * strip.shape[0], strip.shape[1]), strip.dtype),
         ),
-        in_specs=[anywhere] * 3,
-        out_specs=(anywhere,) * 3,
-        scratch_shapes=relay_sems(True) + relay_sems(False) + relay_sems(False)[:4],
+        in_specs=[anywhere] * 2,
+        out_specs=(anywhere,) * 2,
+        scratch_shapes=relay_sems(True) + relay_sems(False),
         compiler_params=params(0),
         cost_estimate=pl.CostEstimate(flops=0, bytes_accessed=100_000_000, transcendentals=0),
-    )(block, table, strip)
+    )(block, table)
     tables = tables.reshape((16,) + table.shape).transpose(1, 0, 2).reshape(table.shape[0], -1)
-    return out.reshape(16 * rows, 2 * width), tables, zone
+    return out.reshape(16 * rows, 2 * width), tables
 
 
 def times(left, weight, out):
@@ -355,12 +348,13 @@
 
 
 def recur_kernel(
-    state, levels, weight, cot_zone, cot_sel, last_sel, final, grad, lefts, rights,
-    xs, us, low, wide, dx, full, last, cot, cot_strip, last_strip, last_zone, end_strip, *sems
+    state, levels, weight, cot_block, cot_sel, last_sel, final, grad, lefts, rights,
+    xs, us, low, wide, dx, full, last, cot, cot_strip, last_strip, last_zone, end_strip, cot_zone, *sems
 ):
     cots, ends = Plane(*sems[:5], sems[5:9]), Plane(*sems[9:14], sems[14:18])
     line = Line(last_strip, last_zone, sems[18:22])
-    lsend, lrecv, rsend, rrecv, esend, erecv = sems[22:]
+    cot_line = Line(cot_block, cot_zone, sems[22:26])
+    lsend, lrecv, rsend, rrecv, esend, erecv = sems[26:]
     core, sibling = line.core, line.sibling
     part, strip, half = last.shape[0], last_strip.shape[1], rights.shape[3]
     mine = pl.ds(pl.multiple_of(core * strip, strip), strip)
@@ -370,24 +364,32 @@
     own_rows = pl.ds(pl.multiple_of(core * part, part), part)
     other_rows = pl.ds(pl.multiple_of((1 - core) * part, part), part)
     enter()
-    cots.first(cot_sel, cot_zone)
+    cot_line.start()
     last[...] = state[...]
     for step in range(3):
         xs[step] = last[...]
         state_f = last[...].astype(jnp.float32)
         low[...] = (state_f * scale_of(state_f)).astype(jnp.bfloat16)
         times(low, weight, us.at[step])
+        if step == 0:
+            cot_line.step(1)
+        if step == 1:
+            cot_line.step(3)
+            cot_line.finish()
+            cots.first(cot_sel, cot_zone)
+        if step == 2:
+            cots.third(cot_strip)
+            push(cot_strip.at[other_rows], cot.at[:, mine], esend.at[0], erecv.at[0], sibling)
+            cot[:, mine] = cot_strip[own_rows, :]
         inner = us[step]
         low[...] = (inner / (1.0 + jnp.exp(-inner))).astype(jnp.bfloat16)
         times_transposed(low, weight, wide)
         active = (levels[...] >= step + 1).astype(jnp.float32)
         last[...] = (last[...].astype(jnp.float32) + active * wide[...]).astype(jnp.bfloat16)
         if step == 0:
+            cot_line.step(2)
+        if step == 1:
             cots.second()
-        if step == 1:
-            cots.third(cot_strip)
-            push(cot_strip.at[other_rows], cot.at[:, mine], esend.at[0], erecv.at[0], sibling)
-            cot[:, mine] = cot_strip[own_rows, :]
     push(last.at[:, theirs], last_strip.at[own_rows], esend.at[1], erecv.at[1], sibling)
     last_strip[own_rows, :] = last[:, mine]
     landed(cot.at[:, theirs], erecv.at[0])
@@ -448,7 +450,7 @@
     landed(final.at[:, theirs], erecv.at[3])
 
 
-def recur(state, levels, weight, cot_zone, cot_sel, last_sel):
+def recur(state, levels, weight, cot_block, cot_sel, last_sel):
     part, width = state.shape
     rows, half, strip = 2 * part, weight.shape[1] // 2, width // 2
     vmem = pl.BlockSpec(memory_space=pltpu.VMEM)
@@ -477,13 +479,14 @@
             pltpu.VMEM((rows, strip), low),
             pltpu.VMEM((4 * rows, strip), low),
             pltpu.VMEM((rows, strip), low),
+            pltpu.VMEM((4 * rows, strip), low),
         ]
         + plane_scratch(rows, strip // 2) * 2
-        + relay_sems(False)[:4]
+        + relay_sems(False)[:4] * 2
         + [dma((6,))] * 4
         + [dma((4,))] * 2,
         compiler_params=params(2),
-    )(state, levels, weight, cot_zone, cot_sel, last_sel)
+    )(state, levels, weight, cot_block, cot_sel, last_sel)
     return final, grad, lefts.reshape(-1, width), rights.reshape(-1, half)
 
 
@@ -677,7 +680,7 @@
     cot_strip = lax.dynamic_slice_in_dim(cotangent, core * strip, strip, 1)
     contract = (((0,), (0,)), ((), ()))
     if lax.axis_size("dp") == 16 and cores == 2:
-        full, tables, cot_zone = gather_weight(weight, destination, cot_strip)
+        full, tables = gather_weight(weight, destination)
         start = me // 4 * 4 * rows
         leaving = lax.dynamic_slice_in_dim(tables[0], start, 4 * rows, 0)
         place = pick(tables[2], pick(tables[1], leaving))
@@ -687,7 +690,7 @@
             state,
             levels.astype(jnp.float32)[:, None],
             full,
-            cot_zone,
+            cot_strip,
             from_column(place, rows, me),
             from_column(source, rows, me),
         )

time: 183 us -> 187 us (1.022)
  Pallas kernels: 170 us -> 173 us
    pallas_call x1, Pallas kernels: 60.3 us -> 77.5 us  [recur(): pl.pallas_call(recur_kernel, out_shape=(jax.ShapeDtypeStruct((rows, width...]
    pallas_call x1, Pallas kernels: 61.1 us -> 48.8 us  [gather_weight(): pl.pallas_call(gather_kernel, out_shape=(jax.ShapeDtypeStruct((4, 2, 2, r...]
where the time goes in v6:
time: 187 us; the launch traced here: 186 us
  Pallas kernels  173 us (93%)
  local copies, waits for them, and re-layouts  7.51 us (4%)
  other arithmetic  5.17 us (3%)
    pallas_call x1, Pallas kernels, recur(): pl.pallas_call(recur_kernel, out_shape=(jax.ShapeDtypeStruct((rows, width...  77.5 us
    pallas_call x1, Pallas kernels, gather_weight(): pl.pallas_call(gather_kernel, out_shape=(jax.ShapeDtypeStruct((4, 2, 2, r...  48.8 us
    pallas_call x1, Pallas kernels, scatter_grad(): pl.pallas_call(scatter_kernel, out_shape=jax.ShapeDtypeStruct((rows, widt...  46.7 us
    unnamed x11, local copies, waits for them, and re-layouts  6.03 us

profile of v6, /device:TPU:0, one launch (start us, length us, event | category | flops | bytes accessed | tf_op | source)
XLA Modules:
  0.0 186.4 jit_solution(11737142824793368163)
XLA Ops:
  0.6 0.0 copy-start
  0.7 0.8 convert_bitcast_fusion
  1.5 0.1 copy.26.levels
  1.6 0.1 copy-done
  1.7 1.0 constant_dynamic-slice_fusion.cot_block
  2.7 0.0 copy-start.2
  2.7 0.9 copy-done.2
  3.6 0.0 copy-start.3
  3.6 0.7 copy-done.3
  4.3 48.8 %shard_map.76 = (bf16[4,2,2,128,2048]{4,3,2,1,0:T(8,128)(2,1)}, s32[4,2,2,3,128]{4,3,2,1,0:T(4,128)S(1)}) custom-call(bf16[128,1024]{1,0:T(8,128)(2,1)S(1)} %copy-done.2, s32[3,128]{1,0:T(4,128)S(1)} %copy-done.3), custom_call_target="tpu_custom_call" | custom-call | bytes 100000000 | tf_op jit(solution)/shard_map/pallas_call | solution.py:314
  53.2 0.7 select_reduce_fusion.2
  53.9 0.1 dynamic_slice.15
  54.0 1.4 select_reduce_fusion.1
  55.3 1.3 select_reduce_fusion
  56.7 0.2 copy.18
  56.8 0.5 fusion.3.cot_sel
  57.3 0.1 copy.22
  57.5 0.5 fusion.7.last_sel
  58.0 77.5 %shard_map.77 = (bf16[128,2048]{1,0:T(8,128)(2,1)S(1)}, bf16[128,2048]{1,0:T(8,128)(2,1)S(1)}, bf16[2,6,64,2048]{3,2,1,0:T(8,128)(2,1)}, bf16[2,6,64,1024]{3,2,1,0:T(8,128)(2,1)S(1)}) custom-call(bf16[64,2048]{1,0:T(8,128)(2,1)S(1)} %constant_dynamic-slice_fusion.1.state, f32[64,1]{1,0:T(8,128)S(1)} %copy.26.levels, bf16[2048,2048]{1,0:T(8,128)(2,1)} %bitcast.16, ...), custom_call_target="tpu_custom_call" | custom-call | tf_op jit(solution)/shard_map/pallas_call | solution.py:459
  135.4 0.0 copy-start.1
  135.4 1.9 %copy-done.1 = bf16[2,6,64,2048]{3,2,1,0:T(8,128)(2,1)S(1)} copy-done((bf16[2,6,64,2048]{3,2,1,0:T(8,128)(2,1)S(1)}, bf16[2,6,64,2048]{3,2,1,0:T(8,128)(2,1)}, u32[]{:S(2)}) %copy-start.1) | copy-done | bytes 3145752
  137.3 46.7 %shard_map.78 = f32[128,1024]{1,0:T(8,128)S(1)} custom-call(bf16[768,2048]{1,0:T(8,128)(2,1)S(1)} %bitcast.13, bf16[768,1024]{1,0:T(8,128)(2,1)S(1)} %bitcast.14), custom_call_target="tpu_custom_call" | custom-call | bytes 100000000 | tf_op jit(solution)/shard_map/pallas_call | solution.py:592
  184.0 0.8 copy.30
  184.8 0.8 copy.31
  185.6 0.8 copy.32
  (3 shorter events, 0.0 us)
Async XLA Ops:
  0.6 1.1 copy-start
  2.7 1.0 copy-start.2
  3.6 0.7 copy-start.3
  135.4 1.9 %copy-start.1 = (bf16[2,6,64,2048]{3,2,1,0:T(8,128)(2,1)S(1)}, bf16[2,6,64,2048]{3,2,1,0:T(8,128)(2,1)}, u32[]{:S(2)}) copy-start(bf16[2,6,64,2048]{3,2,1,0:T(8,128)(2,1)} %get-tuple-element.13) | copy-start | bytes 9437188
